TPU v7x, 256 devices: a whole 4x4x8 slice. The times are simulated.
256 devices in a mesh: blk: 32 (over z, y_lo, core), group: 8 (over y_hi, x).
Axes of the slice: x: 4, y: 4 (y_hi: 2, y_lo: 2; y = y_hi * 2 + y_lo), z: 8, core: 2. Of those that a mesh axis runs over, the one named last changes fastest.
Arguments:
- features: bfloat16 [8, 8192, 2048], P('group', 'blk'), may hold values from -0.29882812 to 0.29882812
- head_weight: bfloat16 [2048, 512], replicated, may hold values from -0.125 to 0.125
- pairs: int32 [8, 8192], P('group', 'blk'), may hold values from 0 to 8191, as said below
Outputs:
- pair_logit: float32 [8, 8192], P('group', 'blk')
- row_lse: float32 [8, 8192], P('group', 'blk')
- proj_grad: float32 [8, 8192, 512], P('group', 'blk')
- head_grad: float32 [2048, 512], replicated
Inputs may be any that keep to these rules, and one draw needn't show every extreme that they name: pairs pairs each view with another view of the same group, and pairs[g, pairs[g, i]] = i.
All inputs are finite; a program needn't handle non-finite values.
Results may differ from a plain program's by a relative error of at most 0.004.
Values may be sent and summed in bfloat16 or wider, within the bound.
A program may use at most 64 MiB of HBM per device.

v0:
```python
import jax
import jax.numpy as jnp
from jax import lax
from jax.sharding import PartitionSpec as P

logit_divisor = 0.1


def tile_scores(sphere_embeddings, partial_block):
    return (
        jnp.einsum(
            "mx,qx->mq", sphere_embeddings, partial_block, preferred_element_type=jnp.float32
        )
        / logit_divisor
    )


def on_device(features, head_weight, pairs):
    feats = features[0]
    partner = pairs[0]
    lines_per_processor = feats.shape[0]
    z = jnp.dot(feats, head_weight, preferred_element_type=jnp.float32)
    inv = lax.rsqrt(jnp.sum(z * z, axis=1) + 1e-06)
    u = z * inv[:, None]
    sphere_embeddings = u.astype(jnp.bfloat16)
    rows_global = lax.axis_index("blk") * lines_per_processor + jnp.arange(
        lines_per_processor, dtype=jnp.int32
    )

    def masked(scores, count):
        cols = jnp.arange(count, dtype=jnp.int32)
        diagonal_exclusion = rows_global[:, None] == cols[None, :]
        pairmask = partner[:, None] == cols[None, :]
        expo = jnp.where(diagonal_exclusion, jnp.zeros_like(scores), jnp.exp(scores))
        return (expo, pairmask)

    partial_block = lax.all_gather(sphere_embeddings, "blk", axis=0, tiled=True)
    scores = tile_scores(sphere_embeddings, partial_block)
    expo, pairmask = masked(scores, partial_block.shape[0])
    den = jnp.sum(expo, axis=1)
    pos = jnp.sum(jnp.where(pairmask, scores, jnp.zeros_like(scores)), axis=1)
    den_all = lax.all_gather(den, "blk", axis=0, tiled=True)
    partial_block = lax.all_gather(sphere_embeddings, "blk", axis=0, tiled=True)
    count = partial_block.shape[0]
    scores = tile_scores(sphere_embeddings, partial_block)
    expo, pairmask = masked(scores, count)
    linear_map_coefficients = (
        expo / den[:, None] + expo / den_all[None, :] - 2.0 * pairmask.astype(jnp.float32)
    )
    collapsed_total_amount = jnp.dot(
        linear_map_coefficients.astype(jnp.bfloat16),
        partial_block,
        preferred_element_type=jnp.float32,
    )
    rescaled_direction_slope = collapsed_total_amount / logit_divisor
    grad_z = inv[:, None] * (
        rescaled_direction_slope - u * jnp.sum(u * rescaled_direction_slope, axis=1, keepdims=True)
    )
    head_term = jnp.einsum(
        "rh,rp->hp", feats, grad_z.astype(jnp.bfloat16), preferred_element_type=jnp.float32
    )
    head_total = lax.psum(head_term, ("blk", "group"))
    return (pos[None, :], jnp.log(den)[None, :], grad_z[None, :, :], head_total)


def solution(mesh):
    in_specs = (P("group", "blk", None), P(), P("group", "blk"))
    out_specs = (P("group", "blk"), P("group", "blk"), P("group", "blk", None), P())
    return jax.shard_map(
        on_device, mesh=mesh, in_specs=in_specs, out_specs=out_specs, check_vma=False
    )
```

profile of v0, /device:TPU:1, one launch (start us, length us, event | category | flops | bytes accessed | tf_op | source)
XLA Modules:
  0.0 413.4 jit_solution(14445626826369091062)
XLA Ops:
  7.2 0.0 copy-start
  7.2 0.0 all-gather.3.cloned.1.call-start
  7.2 1.5 copy-done
  8.8 2.0 multiply_reduce_fusion.1
  10.8 0.8 multiply_convert_fusion
  11.6 0.0 all-gather.3.cloned.1.call-update
  11.6 0.0 all-reduce.2.cloned.1.call-start
  11.7 76.6 %all-gather.3.cloned.1.call-done = bf16[8192,512]{1,0:T(8,128)(2,1)} async-done(((bf16[256,512]{1,0:T(8,128)(2,1)}), bf16[8192,512]{1,0:T(8,128)(2,1)}) %all-gather.3.cloned.1.call-update) | async-done | bytes 8388624 | tf_op jit(solution)/shard_map/all_gather | solution.py:37
  88.3 0.0 copy-start.2
  88.3 0.0 copy-start.3
  88.3 7.7 %fusion = (f32[256]{0:T(256)S(1)}, f32[256]{0:T(256)}, f32[256,8192]{1,0:T(8,128)S(1)}) fusion(s32[256]{0:T(256)S(1)} %iota_add_fusion, s32[256]{0:T(256)} %bitcast.23, bf16[256,512]{1,0:T(8,128)(2,1)} %multiply_convert_fusion, bf16[8192,512]{1,0:T(8,128)(2,1)} %all-gather.3.cloned.1.call-done), kind=kOutput, calls=%fused_computation.6 | convolution fusion | flops 2162163200 | bytes 17043456 | tf_op jit(solution)/shard_map/mx,qx->mq/dot_general | solution.py:11
  96.0 33.0 %all-gather = f32[32,1,256]{2,1,0:T(1,128)S(1)} all-gather(f32[1,1,256]{2,1,0:T(1,128)S(1)} %bitcast.21), channel_id=1, replica_groups=mesh['blk'=32,'group'=8] {'blk'}, dimensions={0}, use_global_device_ids=true | all-gather | bytes 33792 | tf_op jit(solution)/shard_map/all_gather | solution.py:42
  129.0 0.0 copy-done.2
  129.0 0.0 copy-done.3
  129.0 0.0 copy-start.1
  129.0 4.0 multiply_reduce_fusion
  133.0 0.0 copy-done.1
  133.0 2.9 convolution_bitcast_fusion
  135.9 0.0 all-reduce.2.cloned.1.call-update
  135.9 0.6 log.13
  136.5 1.0 fusion.9
  137.5 263.7 %all-reduce.2.cloned.1.call-done = f32[2048,512]{0,1:T(8,128)} async-done(((f32[2048,512]{0,1:T(8,128)}), f32[2048,512]{0,1:T(8,128)}) %all-reduce.2.cloned.1.call-update) | async-done | bytes 4194320 | tf_op jit(solution)/shard_map/psum | solution.py:62
  401.2 5.3 %copy.8 = f32[2048,512]{1,0:T(8,128)} copy(f32[2048,512]{0,1:T(8,128)} %all-reduce.2.cloned.1.call-done) | data formatting | bytes 8388608
  (2 shorter events, 0.0 us)
Async XLA Ops:
  7.2 1.6 copy-start
  7.2 81.1 %all-gather.3.cloned.1.call-start = ((), (), s32[]{:S(2)}) async-start(), calls=%async_computation | async-start | bytes 8650752 | tf_op jit(solution)/shard_map/all_gather | solution.py:37
  11.6 389.6 %all-reduce.2.cloned.1.call-start = ((), (), s32[]{:S(2)}) async-start(), calls=%async_computation.1 | async-start | bytes 8388608 | tf_op jit(solution)/shard_map/psum | solution.py:62
  88.3 40.7 %copy-start.2 = (bf16[8192,512]{1,0:T(8,128)(2,1)S(1)}, bf16[8192,512]{1,0:T(8,128)(2,1)}, u32[]{:S(2)}) copy-start(bf16[8192,512]{1,0:T(8,128)(2,1)} %all-gather.3.cloned.1.call-done) | copy-start | bytes 25165828
  88.3 40.7 %copy-start.3 = (s32[1,256]{1,0:T(1,128)S(1)}, s32[1,256]{1,0:T(1,128)}, u32[]{:S(2)}) copy-start(s32[1,256]{1,0:T(1,128)} %param.5) | copy-start | bytes 3076
  129.0 4.0 copy-start.1
Sparse Core Ops, SparseCore 0:
  11.7 76.4 all-gather.2
  136.1 265.0 all-reduce.1
where the time goes:
time: 414 us; the launch traced here: 413 us
  waiting for transfers between devices  340 us (82%)
  blocking collectives  33 us (8%)
  matrix products  16.6 us (4%)
  between operations  14.1 us (3%)
  local copies, waits for them, and re-layouts  7.46 us (2%)
    psum x1, waiting for transfers between devices, on_device(): head_total = lax.psum(head_term, ('blk', 'group'))  264 us
    all_gather x1, waiting for transfers between devices, on_device(): partial_block = lax.all_gather(sphere_embeddings, 'blk', axis=0, tiled=True)  76.6 us
    all_gather x1, blocking collectives, on_device(): den_all = lax.all_gather(den, 'blk', axis=0, tiled=True)  33 us
  transfers between devices with their start and end apart: 2, of which 2 were waited for; matrix products, arithmetic and copies ran while one was open for 0% of the time, Pallas kernels for 0%

commit v1 on v0

v1 whole, which is shorter than its diff:
```python
import functools

import jax
import jax.numpy as jnp
from jax import lax
from jax.experimental import pallas as pl
from jax.experimental.pallas import tpu as pltpu
from jax.sharding import PartitionSpec as P

MESH = pl.DeviceIdType.MESH
F32 = jnp.float32
BF16 = jnp.bfloat16

HID = 2048
PROJ = 512
ROWS = 256
NZ = 8
NA = 144
NB = ROWS - NA
INV_TEMP = 10.0
LOG2E = 1.4426950408889634

LAST = (
    ((0, 80), (80, 64)),
    ((NA, 48), (NA + 48, 64)),
    ((NA, 64), (NA + 64, 48)),
)


def kernel(
    feat_ref, w_ref, pairs_ref,
    pos_ref, lse_ref, dz_ref, head_ref,
    ub_all, e_all, u_s, inv_s, pcol_s, den_s, pos_s, rden_all, acc_s,
    f_sib, f_t, dzb, pf, sb1, r1, qf, r2, zb, r3, gz,
    z_send, z_recv, y_send, y_recv, c_send, c_recv, d_send, d_recv,
    x_send, x_recv, s1_send, s1_recv, s2_send, s2_recv, s3_send, s3_recv,
    g3_send, g3_recv, g2_send, g2_recv, g1_send, g1_recv, gc_send, gc_recv,
):
    blk = lax.axis_index("blk")
    grp = lax.axis_index("group")
    z, yl, c = blk // 4, lax.rem(blk // 2, 2), lax.rem(blk, 2)
    yh, x = grp // 4, lax.rem(grp, 4)
    y = yh * 2 + yl

    def dev(z_, y_, c_, x_):
        return ((z_ * 2 + lax.rem(y_, 2)) * 2 + c_, (y_ // 2) * 4 + x_)

    def copy(src, dst, ssem, rsem, to):
        return pltpu.make_async_remote_copy(
            src_ref=src, dst_ref=dst, send_sem=ssem, recv_sem=rsem,
            device_id=to, device_id_type=MESH,
        )

    sib = dev(z, y, 1 - c, x)
    ynb = (blk + 2 - 4 * yl, grp)

    barrier = pltpu.get_barrier_semaphore()

    def greet(i, carry):
        pl.semaphore_signal(
            barrier, inc=1, device_id=(lax.rem(blk + i, 32), grp), device_id_type=MESH
        )
        return carry

    lax.fori_loop(1, 32, greet, 0)
    for d in (1, 2, 3):
        pl.semaphore_signal(
            barrier, inc=1, device_id=dev(z, y, c, lax.rem(x + d, 4)), device_id_type=MESH
        )
    for yl_ in (0, 1):
        pl.semaphore_signal(
            barrier, inc=1, device_id=dev(z, (1 - yh) * 2 + yl_, c, x), device_id_type=MESH
        )

    zz = jnp.dot(feat_ref[...], w_ref[...], preferred_element_type=F32)
    inv = lax.rsqrt(jnp.sum(zz * zz, axis=1, keepdims=True) + 1e-06)
    u = zz * inv
    inv_s[...] = inv
    u_s[...] = u
    row0 = pl.multiple_of((yl * 2 + c) * ROWS, ROWS)
    ub_all[z, pl.ds(row0, ROWS), :] = u.astype(BF16)
    pl.semaphore_wait(barrier, 36)

    def origin(dr, s):
        return lax.rem(z + NZ + (-s if dr == 0 else s), NZ)

    def rows_of(yl_, c_, off, n):
        return pl.ds(pl.multiple_of((yl_ * 2 + c_) * ROWS + off, 16), n)

    def piece(zo, yl_, c_, off, n):
        return ub_all.at[zo, rows_of(yl_, c_, off, n), :]

    def z_copy(dr, s, kind):
        off, n = LAST[kind][dr] if s == 3 else ((0, NA) if kind == 0 else (NA, NB))
        ref = piece(origin(dr, s), 1 - yl if kind == 2 else yl, c, off, n)
        to = dev(lax.rem(z + (1 if dr == 0 else NZ - 1), NZ), y, c, x)
        return copy(ref, ref, z_send.at[dr, s, kind], z_recv.at[dr, s, kind], to)

    def z_arrived(dr, s, kind):
        off, n = LAST[kind][dr] if s == 3 else ((0, NA) if kind == 0 else (NA, NB))
        ref = piece(origin(dr, s + 1), 1 - yl if kind == 2 else yl, c, off, n)
        to = dev(lax.rem(z + (1 if dr == 0 else NZ - 1), NZ), y, c, x)
        return copy(ref, ref, z_send.at[dr, s, kind], z_recv.at[dr, s, kind], to)

    def y_ref(i, yl_):
        if i == 0:
            return piece(z, yl_, c, NA, NB)
        if i == 1:
            return piece(z, yl_, c, 0, NA)
        if i < 8:
            return piece(origin((i - 2) // 3, (i - 2) % 3 + 1), yl_, c, 0, NA)
        off, n = LAST[0][i - 8]
        return piece(origin(0, 4), yl_, c, off, n)

    def y_copy(i):
        ref = y_ref(i, yl)
        return copy(ref, ref, y_send.at[i], y_recv.at[i], ynb)

    def y_arrived(i):
        ref = y_ref(i, 1 - yl)
        return copy(ref, ref, y_send.at[i], y_recv.at[i], ynb)

    def c_ref(dr, s, other_y, c_):
        return piece(origin(dr, s), 1 - yl if other_y else yl, c_, 0, ROWS)

    def c_copy(dr, s, other_y):
        ref = c_ref(dr, s, other_y, c)
        i = (s * 2 + dr) * 2 + other_y
        return copy(ref, ref, c_send.at[i], c_recv.at[i], sib)

    def c_arrived(dr, s, other_y):
        ref = c_ref(dr, s, other_y, 1 - c)
        i = (s * 2 + dr) * 2 + other_y
        return copy(ref, ref, c_send.at[i], c_recv.at[i], sib)

    sent = []

    def go(cp):
        cp.start()
        sent.append(cp)

    go(y_copy(0))
    for dr in (0, 1):
        go(z_copy(dr, 0, 0))
    for dr in (0, 1):
        go(z_copy(dr, 0, 1))
    go(y_copy(1))
    go(c_copy(0, 0, 0))
    mine = pl.multiple_of(c * (HID // 2), HID // 2)
    theirs = pl.multiple_of((1 - c) * (HID // 2), HID // 2)
    xcp = copy(feat_ref.at[:, pl.ds(theirs, HID // 2)], f_sib, x_send.at[0], x_recv.at[0], sib)
    go(xcp)

    pcol_s[...] = jnp.broadcast_to(pairs_ref[...], (128, ROWS)).T[:, :1]
    den_s[...] = jnp.zeros_like(den_s)
    pos_s[...] = jnp.zeros_like(pos_s)
    own_row = blk * ROWS + lax.broadcasted_iota(jnp.int32, (ROWS, 1), 0)

    def scores(zo, j):
        block = ub_all[zo, pl.ds(pl.multiple_of(j * ROWS, ROWS), ROWS), :]
        mine_ub = ub_all[z, pl.ds(row0, ROWS), :]
        s = lax.dot_general(
            mine_ub, block, (((1,), (1,)), ((), ())), preferred_element_type=F32
        )
        cols = (zo * 4 + j) * ROWS + lax.broadcasted_iota(jnp.int32, (ROWS, ROWS), 1)
        e = jnp.where(cols == own_row, 0.0, jnp.exp2(s * (INV_TEMP * LOG2E)))
        e_all[zo, :, pl.ds(pl.multiple_of(j * ROWS, ROWS), ROWS)] = e
        p = jnp.where(cols == pcol_s[...], s, 0.0)
        den_s[...] += e[:, :128] + e[:, 128:]
        pos_s[...] += p[:, :128] + p[:, 128:]

    def scores_of(zo):
        def body(j, carry):
            scores(zo, j)
            return carry

        lax.fori_loop(0, 4, body, 0)

    y_arrived(0).wait_recv()
    for dr in (0, 1):
        go(z_copy(dr, 0, 2))
    f_t[:, :ROWS] = feat_ref[:, pl.ds(mine, HID // 2)].T
    y_arrived(1).wait_recv()
    go(c_copy(0, 0, 1))
    xcp.wait_recv()
    f_t[:, ROWS:] = f_sib[...].T

    for s in (1, 2, 3, 4):
        drs = (0, 1)
        for kind in (0, 1, 2):
            for dr in drs:
                z_arrived(dr, s - 1, kind).wait_recv()
                if s < 4:
                    go(z_copy(dr, s, kind))
                if kind == 0:
                    go(y_copy(2 + dr * 3 + s - 1) if s < 4 else y_copy(8 + dr))
            if kind == 1:
                for dr in drs if s < 4 else (0,):
                    go(c_copy(dr, s, 0))
        for dr in drs if s > 1 else (0,):
            for oy in (0, 1):
                c_arrived(dr, s - 1, oy).wait_recv()
            scores_of(origin(dr, s - 1))
        for dr in drs:
            y_arrived(2 + dr * 3 + s - 1 if s < 4 else 8 + dr).wait_recv()
            if s < 4 or dr == 1:
                go(c_copy(dr if s < 4 else 0, s, 1))
    for oy in (0, 1):
        c_arrived(0, 4, oy).wait_recv()
    scores_of(origin(0, 4))

    den = jnp.sum(den_s[...], axis=1, keepdims=True)
    r_own = 1.0 / den
    rden_all[blk] = jnp.broadcast_to(r_own, (ROWS, 128)).T[:1, :]

    def d_copy(dz_, k):
        to_blk = lax.rem(z + dz_, NZ) * 4 + lax.rem(yl + k // 2, 2) * 2 + lax.rem(c + k % 2, 2)
        i = dz_ * 4 + k
        return copy(
            rden_all.at[blk], rden_all.at[blk], d_send.at[i], d_recv.at[i], (to_blk, grp)
        )

    def d_arrived(dz_, k):
        i = dz_ * 4 + k
        from_blk = (
            lax.rem(z + NZ - dz_, NZ) * 4
            + lax.rem(yl + k // 2, 2) * 2
            + lax.rem(c + k % 2, 2)
        )
        ref = rden_all.at[from_blk]
        return copy(ref, ref, d_send.at[i], d_recv.at[i], (blk, grp))

    for dz_ in (4, 3, 5, 2, 6, 1, 7, 0):
        for k in range(4):
            if dz_ or k:
                go(d_copy(dz_, k))

    lse_ref[...] = jnp.broadcast_to(jnp.log(den), (ROWS, 128)).T[:1, :]
    pos = jnp.sum(pos_s[...], axis=1, keepdims=True) * INV_TEMP
    pos_ref[...] = jnp.broadcast_to(pos, (ROWS, 128)).T[:1, :]

    for n, dz_ in enumerate((0, 1, 7, 2, 6, 3, 5, 4)):
        for k in range(4):
            if dz_ or k:
                d_arrived(dz_, k).wait_recv()
        zo = lax.rem(z + NZ - dz_, NZ)
        parts = []
        for j in range(4):
            cols = (zo * 4 + j) * ROWS + lax.broadcasted_iota(jnp.int32, (ROWS, ROWS), 1)
            e = e_all[zo, :, j * ROWS : (j + 1) * ROWS]
            h = e * (r_own + rden_all[zo * 4 + j]) - jnp.where(cols == pcol_s[...], 2.0, 0.0)
            parts.append(h.astype(BF16))
        g = jnp.dot(
            jnp.concatenate(parts, axis=1), ub_all[zo], preferred_element_type=F32
        )
        if n == 0:
            acc_s[...] = g
        else:
            acc_s[...] += g

    slope = acc_s[...] * INV_TEMP
    u = u_s[...]
    dz = inv_s[...] * (slope - u * jnp.sum(u * slope, axis=1, keepdims=True))
    dz_ref[...] = dz
    dzb[0] = dz.astype(BF16)
    xcp = copy(dzb.at[0], dzb.at[1], x_send.at[1], x_recv.at[1], sib)
    go(xcp)
    xcp.wait_recv()

    def along(t, first, d):
        if (t % 2 == 0) == first:
            return dev(z, y, c, lax.rem(x + d, 4))
        return dev(z, lax.rem(y + d, 4), c, x)

    def place(t, first):
        return x if (t % 2 == 0) == first else y

    def s1_copy(t, d):
        j = lax.rem(place(t, True) + d, 4)
        return copy(sb1.at[t, j], r1.at[t, d - 1], s1_send.at[t, d - 1], s1_recv.at[t, d - 1], along(t, True, d))

    def s2_copy(t, d):
        j = lax.rem(place(t, False) + d, 4)
        return copy(qf.at[t, j], r2.at[t, d - 1], s2_send.at[t, d - 1], s2_recv.at[t, d - 1], along(t, False, d))

    def zslice(ref, p, j):
        return ref.at[p, :, pl.ds(pl.multiple_of((j // 4) * 8, 8), 8), pl.ds(pl.multiple_of(lax.rem(j, 4) * 128, 128), 128)]

    def zpeer(d):
        return dev(lax.rem(z + d, NZ), y, c, x)

    def s3_copy(p, d):
        j = lax.rem(z + d, NZ)
        return copy(zslice(zb, p, j), r3.at[p, d - 1], s3_send.at[p, d - 1], s3_recv.at[p, d - 1], zpeer(d))

    def g3_copy(p, d, mine_=True):
        ref = zslice(gz, p, z if mine_ else lax.rem(z + NZ - d, NZ))
        return copy(ref, ref, g3_send.at[p, d - 1], g3_recv.at[p, d - 1], zpeer(d))

    def out_rows(t, a, b, n):
        start = c * (HID // 2) + t * 256 + a * 64 + b * 16
        return head_ref.at[pl.ds(pl.multiple_of(start, 16), n), :]

    def g2_copy(t, d, mine_=True):
        b = place(t, False)
        ref = out_rows(t, place(t, True), b if mine_ else lax.rem(b + 4 - d, 4), 16)
        return copy(ref, ref, g2_send.at[t, d - 1], g2_recv.at[t, d - 1], along(t, False, d))

    def g1_copy(t, d, mine_=True):
        a = place(t, True)
        ref = out_rows(t, a if mine_ else lax.rem(a + 4 - d, 4), 0, 64)
        return copy(ref, ref, g1_send.at[t, d - 1], g1_recv.at[t, d - 1], along(t, True, d))

    def gc_copy(t, d):
        a = place(t, True)
        ref = out_rows(t, lax.rem(a + 4 - d, 4), 0, 64)
        return copy(ref, ref, gc_send.at[t, d], gc_recv.at[t, d], sib)

    def gc_arrived(t, d):
        start = (1 - c) * (HID // 2) + t * 256 + lax.rem(place(t, True) + 4 - d, 4) * 64
        ref = head_ref.at[pl.ds(pl.multiple_of(start, 64), 64), :]
        return copy(ref, ref, gc_send.at[t, d], gc_recv.at[t, d], sib)

    D3, D7 = (2, 1, 3), (4, 3, 5, 2, 6, 1, 7)

    def stage1(t):
        dzs = jnp.concatenate([dzb[0], dzb[1]], axis=0)
        part = jnp.dot(f_t[t * 256 : (t + 1) * 256, :], dzs, preferred_element_type=F32)
        pf[t] = part.reshape(4, 64, PROJ)
        sb1[t] = part.astype(BF16).reshape(4, 64, PROJ)
        for d in D3:
            go(s1_copy(t, d))

    def stage2(t):
        for d in D3:
            s1_copy(t, d).wait_recv()
        total = pf[t, place(t, True)]
        for d in range(3):
            total = total + r1[t, d].astype(F32)
        qf[t] = total.reshape(4, 16, PROJ)
        for d in D3:
            go(s2_copy(t, d))

    def stage3(p):
        for i in (0, 1):
            t = 2 * p + i
            for d in D3:
                s2_copy(t, d).wait_recv()
            zb[p, i] = qf[t, place(t, False)] + r2[t, 0] + r2[t, 1] + r2[t, 2]
        for d in D7:
            go(s3_copy(p, d))

    def stage4(p):
        for d in D7:
            s3_copy(p, d).wait_recv()
        rows = pl.ds(pl.multiple_of((z // 4) * 8, 8), 8)
        cols = pl.ds(pl.multiple_of(lax.rem(z, 4) * 128, 128), 128)
        total = zb[p, :, rows, cols]
        for d in range(7):
            total = total + r3[p, d]
        gz[p, :, rows, cols] = total
        for d in D7:
            go(g3_copy(p, d))

    def stage5(p):
        for d in D7:
            g3_copy(p, d, False).wait_recv()
        for i in (0, 1):
            t = 2 * p + i
            start = c * (HID // 2) + t * 256 + place(t, True) * 64 + place(t, False) * 16
            head_ref[pl.ds(pl.multiple_of(start, 16), 16), :] = gz[p, i].astype(BF16)
            for d in D3:
                go(g2_copy(t, d))

    def stage6(t):
        for d in D3:
            g2_copy(t, d, False).wait_recv()
        for d in D3:
            go(g1_copy(t, d))
        go(gc_copy(t, 0))

    def stage7(t):
        for d in D3:
            g1_copy(t, d, False).wait_recv()
            go(gc_copy(t, d))

    for t in range(4):
        stage1(t)
    stage2(0)
    stage2(1)
    stage3(0)
    stage2(2)
    stage2(3)
    stage4(0)
    stage3(1)
    stage5(0)
    stage4(1)
    stage6(0)
    stage6(1)
    stage5(1)
    stage6(2)
    stage6(3)
    for t in range(4):
        stage7(t)
    for t in range(4):
        for d in range(4):
            gc_arrived(t, d).wait_recv()
    for cp in sent:
        cp.wait_send()


def on_device(features, head_weight, pairs):
    vmem = pl.BlockSpec(memory_space=pltpu.VMEM)
    dma = pltpu.SemaphoreType.DMA
    pos, lse, dz, head = pl.pallas_call(
        kernel,
        out_shape=(
            jax.ShapeDtypeStruct((1, ROWS), F32),
            jax.ShapeDtypeStruct((1, ROWS), F32),
            jax.ShapeDtypeStruct((ROWS, PROJ), F32),
            jax.ShapeDtypeStruct((HID, PROJ), BF16),
        ),
        in_specs=[vmem] * 3,
        out_specs=(vmem,) * 4,
        scratch_shapes=[
            pltpu.VMEM((NZ, 4 * ROWS, PROJ), BF16),
            pltpu.VMEM((NZ, ROWS, 4 * ROWS), F32),
            pltpu.VMEM((ROWS, PROJ), F32),
            pltpu.VMEM((ROWS, 1), F32),
            pltpu.VMEM((ROWS, 1), jnp.int32),
            pltpu.VMEM((ROWS, 128), F32),
            pltpu.VMEM((ROWS, 128), F32),
            pltpu.VMEM((32, 1, ROWS), F32),
            pltpu.VMEM((ROWS, PROJ), F32),
            pltpu.VMEM((ROWS, HID // 2), BF16),
            pltpu.VMEM((HID // 2, 2 * ROWS), BF16),
            pltpu.VMEM((2, ROWS, PROJ), BF16),
            pltpu.VMEM((4, 4, 64, PROJ), F32),
            pltpu.VMEM((4, 4, 64, PROJ), BF16),
            pltpu.VMEM((4, 3, 64, PROJ), BF16),
            pltpu.VMEM((4, 4, 16, PROJ), F32),
            pltpu.VMEM((4, 3, 16, PROJ), F32),
            pltpu.VMEM((2, 2, 16, PROJ), F32),
            pltpu.VMEM((2, 7, 2, 8, 128), F32),
            pltpu.VMEM((2, 2, 16, PROJ), F32),
            dma((2, 4, 3)), dma((2, 4, 3)),
            dma((10,)), dma((10,)),
            dma((20,)), dma((20,)),
            dma((32,)), dma((32,)),
            dma((2,)), dma((2,)),
            dma((4, 3)), dma((4, 3)),
            dma((4, 3)), dma((4, 3)),
            dma((2, 7)), dma((2, 7)),
            dma((2, 7)), dma((2, 7)),
            dma((4, 3)), dma((4, 3)),
            dma((4, 3)), dma((4, 3)),
            dma((4, 4)), dma((4, 4)),
        ],
        compiler_params=pltpu.CompilerParams(
            collective_id=0, has_side_effects=True, vmem_limit_bytes=60 << 20
        ),
        name="ntxent",
    )(features[0], head_weight, pairs)
    return pos, lse, dz[None], head.astype(F32)


def solution(mesh):
    in_specs = (P("group", "blk", None), P(), P("group", "blk"))
    out_specs = (P("group", "blk"), P("group", "blk"), P("group", "blk", None), P())
    return jax.shard_map(
        on_device, mesh=mesh, in_specs=in_specs, out_specs=out_specs, check_vma=False
    )
```

time: 414 us -> 105 us (0.25)
  waiting for transfers between devices: 340 us -> 0 us
  Pallas kernels: 0 us -> 98.3 us
  blocking collectives: 33 us -> 0 us
  matrix products: 16.6 us -> 0 us
  between operations: 14.1 us -> 0.67 us
  local copies, waits for them, and re-layouts: 7.46 us -> 1.93 us
    psum x1 -> x0, waiting for transfers between devices: 264 us -> none  [on_device(): head_total = lax.psum(head_term, ('blk', 'group'))]
    pallas_call x0 -> x1, Pallas kernels: none -> 98.3 us  [on_device(): pl.pallas_call(kernel, out_shape=(jax.ShapeDtypeStruct((1, ROWS), F32), j...]
    all_gather x1 -> x0, waiting for transfers between devices: 76.6 us -> none  [on_device(): partial_block = lax.all_gather(sphere_embeddings, 'blk', axis=0, tiled=True)]
    all_gather x1 -> x0, blocking collectives: 33 us -> none  [on_device(): den_all = lax.all_gather(den, 'blk', axis=0, tiled=True)]
    dot_general x4 -> x0, matrix products: 16.6 us -> none  [the longest x1 7.69 us: tile_scores(): jnp.einsum('mx,qx->mq', sphere_embeddings, partial_block, preferred_eleme...]
    unnamed x9, local copies, waits for them, and re-layouts: 6.89 us -> 1.93 us
  transfers between devices with their start and end apart: 2 -> 0, of which waited for: 2 -> 0; matrix products, arithmetic and copies ran while one was open for 0% -> 0% of each run, Pallas kernels for 0% -> 0%
where the time goes in v1:
time: 105 us
  Pallas kernels  98.3 us (94%)
  other arithmetic  4.26 us (4%)
  local copies, waits for them, and re-layouts  1.93 us (2%)
    pallas_call x1, Pallas kernels, on_device(): pl.pallas_call(kernel, out_shape=(jax.ShapeDtypeStruct((1, ROWS), F32), j...  98.3 us
    convert_element_type x1, other arithmetic, on_device(): return (pos, lse, dz[None], head.astype(F32))  4.26 us

profile of v1, /device:TPU:1, one launch (start us, length us, event | category | flops | bytes accessed | tf_op | source)
XLA Modules:
  0.0 105.1 jit_solution(17594225463525906601)
XLA Ops:
  0.6 98.3 %ntxent.1 = (f32[1,256]{1,0:T(1,128)}, f32[1,256]{1,0:T(1,128)}, f32[256,512]{1,0:T(8,128)}, bf16[2048,512]{1,0:T(8,128)(2,1)}) custom-call(bf16[256,2048]{1,0:T(8,128)(2,1)} %bitcast.2, bf16[2048,512]{1,0:T(8,128)(2,1)} %w_ref.1, s32[1,256]{1,0:T(1,128)} %pairs_ref.1), custom_call_target="tpu_custom_call" | custom-call | tf_op jit(solution)/shard_map/ntxent/pallas_call | solution.py:415
  98.9 0.0 copy-start.2
  98.9 0.0 copy-start.1
  99.0 0.0 copy-start
  99.0 4.3 %convert_element_type.3 = f32[2048,512]{1,0:T(8,128)} convert(bf16[2048,512]{1,0:T(8,128)(2,1)} %get-tuple-element.11) | non-fusion elementwise | flops 1048576 | bytes 6291456 | tf_op jit(solution)/shard_map/convert_element_type | solution.py:464
  103.2 0.0 copy-done.2
  103.2 0.6 copy.10
  103.8 0.0 copy-done.1
  103.8 0.6 copy.11
  104.4 0.0 copy-done
  104.4 0.8 copy.12
Async XLA Ops:
  98.9 4.3 %copy-start.2 = (f32[1,256]{1,0:T(1,128)S(1)}, f32[1,256]{1,0:T(1,128)}, u32[]{:S(2)}) copy-start(f32[1,256]{1,0:T(1,128)} %get-tuple-element.16) | copy-start | bytes 3076
  98.9 4.8 %copy-start.1 = (f32[1,256]{1,0:T(1,128)S(1)}, f32[1,256]{1,0:T(1,128)}, u32[]{:S(2)}) copy-start(f32[1,256]{1,0:T(1,128)} %get-tuple-element.17) | copy-start | bytes 3076
  99.0 5.4 %copy-start = (f32[256,512]{1,0:T(8,128)S(1)}, f32[256,512]{1,0:T(8,128)}, u32[]{:S(2)}) copy-start(f32[256,512]{1,0:T(8,128)} %get-tuple-element.10) | copy-start | bytes 1572868

commit v2 on v1

v2 whole, which is shorter than its diff:
```python
import functools

import jax
import jax.numpy as jnp
from jax import lax
from jax.experimental import pallas as pl
from jax.experimental.pallas import tpu as pltpu
from jax.sharding import PartitionSpec as P

MESH = pl.DeviceIdType.MESH
F32 = jnp.float32
BF16 = jnp.bfloat16

HID = 2048
PROJ = 512
ROWS = 256
NZ = 8
NA = (176, 160)
INV_TEMP = 10.0
LOG2E = 1.4426950408889634

LAST = (((0, 144), (144, 112)), ((128, 128), (0, 128)))


def kernel(
    feat_ref, w_ref, pairs_ref,
    pos_ref, lse_ref, dz_ref, head_ref,
    ub_all, e_all, u_s, inv_s, pcol_s, den_s, pos_s, rden_all, acc_s,
    f_sib, f_t, dzb, pf, sb1, r1, qf, r2, zb, r3, in_sem,
    z_send, z_recv, y_send, y_recv, c_send, c_recv, d_send, d_recv,
    x_send, x_recv, s1_send, s1_recv, s2_send, s2_recv, s3_send, s3_recv,
    g3_send, g3_recv, g2_send, g2_recv, g1_send, g1_recv, gc_send, gc_recv,
):
    blk = lax.axis_index("blk")
    grp = lax.axis_index("group")
    z, yl, c = blk // 4, lax.rem(blk // 2, 2), lax.rem(blk, 2)
    yh, x = grp // 4, lax.rem(grp, 4)
    y = yh * 2 + yl

    def dev(z_, y_, c_, x_):
        return ((z_ * 2 + lax.rem(y_, 2)) * 2 + c_, (y_ // 2) * 4 + x_)

    def copy(src, dst, ssem, rsem, to):
        return pltpu.make_async_remote_copy(
            src_ref=src, dst_ref=dst, send_sem=ssem, recv_sem=rsem,
            device_id=to, device_id_type=MESH,
        )

    sib = dev(z, y, 1 - c, x)
    ynb = (blk + 2 - 4 * yl, grp)

    barrier = pltpu.get_barrier_semaphore()
    ring = (
        dev(z, y, c, lax.rem(x + 1, 4)),
        dev(z, y, c, lax.rem(x + 3, 4)),
        dev(z, lax.rem(y + 1, 4), c, x),
        dev(z, lax.rem(y + 3, 4), c, x),
    )
    znext = (dev(lax.rem(z + 1, NZ), y, c, x), dev(lax.rem(z + NZ - 1, NZ), y, c, x))
    for to in znext + (sib,) + ring:
        pl.semaphore_signal(barrier, inc=1, device_id=to, device_id_type=MESH)

    zz = jnp.dot(feat_ref[...], w_ref[...], preferred_element_type=F32)
    inv = lax.rsqrt(jnp.sum(zz * zz, axis=1, keepdims=True) + 1e-06)
    u = zz * inv
    inv_s[...] = inv
    u_s[...] = u
    row0 = pl.multiple_of((yl * 2 + c) * ROWS, ROWS)
    ub_all[z, pl.ds(row0, ROWS), :] = u.astype(BF16)
    pl.semaphore_wait(barrier, 7)

    def origin(dr, s):
        return lax.rem(z + NZ + (-s if dr == 0 else s), NZ)

    def rows_of(yl_, c_, off, n):
        return pl.ds(pl.multiple_of((yl_ * 2 + c_) * ROWS + off, 16), n)

    def piece(zo, yl_, c_, off, n):
        return ub_all.at[zo, rows_of(yl_, c_, off, n), :]

    def z_ref(dr, s, kind, zo):
        if s == 3:
            return piece(zo, 1 - yl if kind else yl, c, *LAST[kind][dr])
        na = NA[dr]
        return piece(zo, 1 - yl if kind == 2 else yl, c, *((na, ROWS - na) if kind else (0, na)))

    def z_copy(dr, s, kind):
        ref = z_ref(dr, s, kind, origin(dr, s))
        return copy(ref, ref, z_send.at[dr, s, kind], z_recv.at[dr, s, kind], znext[dr])

    def z_arrived(dr, s, kind):
        ref = z_ref(dr, s, kind, origin(dr, s + 1))
        return copy(ref, ref, z_send.at[dr, s, kind], z_recv.at[dr, s, kind], znext[dr])

    def y_ref(dr, s, yl_):
        if s == 0:
            return piece(z, yl_, c, *((NA[1], ROWS - NA[1]) if dr == 0 else (0, NA[1])))
        return piece(origin(dr, s), yl_, c, 0, NA[dr])

    def y_copy(dr, s):
        ref = y_ref(dr, s, yl)
        return copy(ref, ref, y_send.at[dr, s], y_recv.at[dr, s], ynb)

    def y_arrived(dr, s):
        ref = y_ref(dr, s, 1 - yl)
        return copy(ref, ref, y_send.at[dr, s], y_recv.at[dr, s], ynb)

    def c_ref(dr, s, other, c_):
        part = LAST[other][dr] if s == 4 else (0, ROWS)
        return piece(origin(dr, s), 1 - yl if other else yl, c_, *part)

    def c_copy(dr, s, other):
        ref = c_ref(dr, s, other, c)
        return copy(ref, ref, c_send.at[dr, s, other], c_recv.at[dr, s, other], sib)

    def c_arrived(dr, s, other):
        ref = c_ref(dr, s, other, 1 - c)
        return copy(ref, ref, c_send.at[dr, s, other], c_recv.at[dr, s, other], sib)

    sent = []

    def go(cp):
        cp.start()
        sent.append(cp)

    def flush():
        for cp in sent:
            cp.wait_send()
        sent.clear()

    go(y_copy(0, 0))
    for kind in (0, 1):
        for dr in (0, 1):
            go(z_copy(dr, 0, kind))
    go(y_copy(1, 0))
    go(c_copy(0, 0, 0))
    for to in ring:
        pl.semaphore_signal(in_sem, inc=1, device_id=to, device_id_type=MESH)
    mine = pl.multiple_of(c * (HID // 2), HID // 2)
    theirs = pl.multiple_of((1 - c) * (HID // 2), HID // 2)
    xcp = copy(feat_ref.at[:, pl.ds(theirs, HID // 2)], f_sib, x_send.at[0], x_recv.at[0], sib)
    go(xcp)

    pcol_s[...] = jnp.broadcast_to(pairs_ref[...], (128, ROWS)).T[:, :1]
    den_s[...] = jnp.zeros_like(den_s)
    pos_s[...] = jnp.zeros_like(pos_s)
    own_row = blk * ROWS + lax.broadcasted_iota(jnp.int32, (ROWS, 1), 0)

    def scores(zo, j):
        block = ub_all[zo, pl.ds(pl.multiple_of(j * ROWS, ROWS), ROWS), :]
        mine_ub = ub_all[z, pl.ds(row0, ROWS), :]
        s = lax.dot_general(
            mine_ub, block, (((1,), (1,)), ((), ())), preferred_element_type=F32
        )
        cols = (zo * 4 + j) * ROWS + lax.broadcasted_iota(jnp.int32, (ROWS, ROWS), 1)
        e = jnp.where(cols == own_row, 0.0, jnp.exp2(s * (INV_TEMP * LOG2E)))
        e_all[zo, :, pl.ds(pl.multiple_of(j * ROWS, ROWS), ROWS)] = e
        p = jnp.where(cols == pcol_s[...], s, 0.0)
        den_s[...] += e[:, :128] + e[:, 128:]
        pos_s[...] += p[:, :128] + p[:, 128:]

    def scores_of(zo):
        def body(j, carry):
            scores(zo, j)
            return carry

        lax.fori_loop(0, 4, body, 0)

    y_arrived(0, 0).wait_recv()
    for dr in (0, 1):
        go(z_copy(dr, 0, 2))
    f_t[:, :ROWS] = feat_ref[:, pl.ds(mine, HID // 2)].T
    y_arrived(1, 0).wait_recv()
    go(c_copy(0, 0, 1))
    xcp.wait_recv()
    f_t[:, ROWS:] = f_sib[...].T

    for s in (1, 2, 3):
        last = s == 3
        for dr in (0, 1):
            z_arrived(dr, s - 1, 0).wait_recv()
            if not last:
                go(z_copy(dr, s, 0))
            elif dr == 0:
                go(z_copy(0, 3, 0))
            go(y_copy(dr, s))
        for dr in (0, 1):
            z_arrived(dr, s - 1, 1).wait_recv()
            if not last:
                go(z_copy(dr, s, 1))
            elif dr == 1:
                go(z_copy(1, 3, 0))
            go(c_copy(dr, s, 0))
        for dr in (0, 1):
            z_arrived(dr, s - 1, 2).wait_recv()
            if not last:
                go(z_copy(dr, s, 2))
        for dr in (0, 1) if s > 1 else (0,):
            for other in (0, 1):
                c_arrived(dr, s - 1, other).wait_recv()
            scores_of(origin(dr, s - 1))
        for dr in (0, 1):
            y_arrived(dr, s).wait_recv()
            if last:
                go(z_copy(dr, 3, 1))
            go(c_copy(dr, s, 1))
    for dr in (0, 1):
        for other in (0, 1):
            c_arrived(dr, 3, other).wait_recv()
        scores_of(origin(dr, 3))
    flush()
    pl.semaphore_wait(in_sem, 4)
    far = origin(0, 4)
    for other in (0, 1):
        for dr in (0, 1):
            z_arrived(dr, 3, other).wait_recv()
            go(c_copy(dr, 4, other))
        scores(far, (1 - yl if other else yl) * 2 + c)
    for other in (0, 1):
        for dr in (0, 1):
            c_arrived(dr, 4, other).wait_recv()
        scores(far, (1 - yl if other else yl) * 2 + 1 - c)

    den = jnp.sum(den_s[...], axis=1, keepdims=True)
    r_own = 1.0 / den
    rden_all[blk] = jnp.broadcast_to(r_own, (ROWS, 128)).T[:1, :]

    def d_copy(dz_, k):
        to_blk = lax.rem(z + dz_, NZ) * 4 + lax.rem(yl + k // 2, 2) * 2 + lax.rem(c + k % 2, 2)
        i = dz_ * 4 + k
        return copy(
            rden_all.at[blk], rden_all.at[blk], d_send.at[i], d_recv.at[i], (to_blk, grp)
        )

    def d_arrived(dz_, k):
        i = dz_ * 4 + k
        from_blk = (
            lax.rem(z + NZ - dz_, NZ) * 4
            + lax.rem(yl + k // 2, 2) * 2
            + lax.rem(c + k % 2, 2)
        )
        ref = rden_all.at[from_blk]
        return copy(ref, ref, d_send.at[i], d_recv.at[i], (blk, grp))

    for dz_ in (4, 3, 5, 2, 6, 1, 7, 0):
        for k in range(4):
            if dz_ or k:
                go(d_copy(dz_, k))

    lse_ref[...] = jnp.broadcast_to(jnp.log(den), (ROWS, 128)).T[:1, :]
    pos = jnp.sum(pos_s[...], axis=1, keepdims=True) * INV_TEMP
    pos_ref[...] = jnp.broadcast_to(pos, (ROWS, 128)).T[:1, :]

    for n, dz_ in enumerate((0, 1, 7, 2, 6, 3, 5, 4)):
        for k in range(4):
            if dz_ or k:
                d_arrived(dz_, k).wait_recv()
        zo = lax.rem(z + NZ - dz_, NZ)
        parts = []
        for j in range(4):
            cols = (zo * 4 + j) * ROWS + lax.broadcasted_iota(jnp.int32, (ROWS, ROWS), 1)
            e = e_all[zo, :, j * ROWS : (j + 1) * ROWS]
            h = e * (r_own + rden_all[zo * 4 + j]) - jnp.where(cols == pcol_s[...], 2.0, 0.0)
            parts.append(h.astype(BF16))
        g = jnp.dot(
            jnp.concatenate(parts, axis=1), ub_all[zo], preferred_element_type=F32
        )
        if n == 0:
            acc_s[...] = g
        else:
            acc_s[...] += g

    slope = acc_s[...] * INV_TEMP
    u = u_s[...]
    dz = inv_s[...] * (slope - u * jnp.sum(u * slope, axis=1, keepdims=True))
    dz_ref[...] = dz
    dzb[0] = dz.astype(BF16)
    xcp = copy(dzb.at[0], dzb.at[1], x_send.at[1], x_recv.at[1], sib)
    go(xcp)
    xcp.wait_recv()

    def along(t, first, d):
        if (t % 2 == 0) == first:
            return dev(z, y, c, lax.rem(x + d, 4))
        return dev(z, lax.rem(y + d, 4), c, x)

    def place(t, first):
        return x if (t % 2 == 0) == first else y

    def s1_copy(t, d):
        j = lax.rem(place(t, True) + d, 4)
        return copy(sb1.at[t, j], r1.at[t, d - 1], s1_send.at[t, d - 1], s1_recv.at[t, d - 1], along(t, True, d))

    def s2_copy(t, d):
        j = lax.rem(place(t, False) + d, 4)
        return copy(qf.at[t, j], r2.at[t, d - 1], s2_send.at[t, d - 1], s2_recv.at[t, d - 1], along(t, False, d))

    def out_rows(t, a, b, n):
        start = c * (HID // 2) + t * 256 + a * 64 + b * 16
        return pl.ds(pl.multiple_of(start, 16), n)

    def zcols(j):
        return pl.ds(pl.multiple_of(lax.rem(j, 2) * 256, 256), 256)

    def zpeer(d):
        return dev(lax.rem(z + d, NZ), y, c, x)

    def s3_copy(d):
        j = lax.rem(z + d, NZ)
        return copy(zb.at[j // 2, :, zcols(j)], r3.at[d - 1], s3_send.at[d - 1], s3_recv.at[d - 1], zpeer(d))

    def zrows(j):
        t = j // 2
        odd = lax.rem(t, 2)
        return out_rows(t, x + odd * (y - x), y + odd * (x - y), 16)

    def g3_copy(d, mine_=True):
        j = z if mine_ else lax.rem(z + NZ - d, NZ)
        ref = head_ref.at[zrows(j), zcols(j)]
        return copy(ref, ref, g3_send.at[d - 1], g3_recv.at[d - 1], zpeer(d))

    def g2_copy(t, d, mine_=True):
        b = place(t, False)
        ref = head_ref.at[out_rows(t, place(t, True), b if mine_ else lax.rem(b + 4 - d, 4), 16), :]
        return copy(ref, ref, g2_send.at[t, d - 1], g2_recv.at[t, d - 1], along(t, False, d))

    def g1_copy(t, d, mine_=True):
        a = place(t, True)
        ref = head_ref.at[out_rows(t, a if mine_ else lax.rem(a + 4 - d, 4), 0, 64), :]
        return copy(ref, ref, g1_send.at[t, d - 1], g1_recv.at[t, d - 1], along(t, True, d))

    def gc_copy(t, d):
        a = place(t, True)
        ref = head_ref.at[out_rows(t, lax.rem(a + 4 - d, 4), 0, 64), :]
        return copy(ref, ref, gc_send.at[t, d], gc_recv.at[t, d], sib)

    def gc_arrived(t, d):
        start = (1 - c) * (HID // 2) + t * 256 + lax.rem(place(t, True) + 4 - d, 4) * 64
        ref = head_ref.at[pl.ds(pl.multiple_of(start, 64), 64), :]
        return copy(ref, ref, gc_send.at[t, d], gc_recv.at[t, d], sib)

    D3, D7 = (2, 1, 3), (4, 3, 5, 2, 6, 1, 7)

    def stage1(t):
        dzs = jnp.concatenate([dzb[0], dzb[1]], axis=0)
        part = jnp.dot(f_t[t * 256 : (t + 1) * 256, :], dzs, preferred_element_type=F32)
        pf[t] = part.reshape(4, 64, PROJ)
        sb1[t] = part.astype(BF16).reshape(4, 64, PROJ)
        for d in D3:
            go(s1_copy(t, d))

    def stage2(t):
        for d in D3:
            s1_copy(t, d).wait_recv()
        total = pf[t, place(t, True)]
        for d in range(3):
            total = total + r1[t, d].astype(F32)
        qf[t] = total.reshape(4, 16, PROJ)
        for d in D3:
            go(s2_copy(t, d))

    def stage3():
        for t in range(4):
            for d in D3:
                s2_copy(t, d).wait_recv()
            zb[t] = qf[t, place(t, False)] + r2[t, 0] + r2[t, 1] + r2[t, 2]
        for d in D7:
            go(s3_copy(d))

    def stage4():
        total = zb[z // 2, :, zcols(z)]
        for d in D7:
            s3_copy(d).wait_recv()
        for d in range(7):
            total = total + r3[d]
        head_ref[zrows(z), zcols(z)] = total.astype(BF16)
        for d in D7:
            go(g3_copy(d))

    def stage5():
        for d in D7:
            g3_copy(d, False).wait_recv()
        for t in range(4):
            for d in D3:
                go(g2_copy(t, d))

    def stage6(t):
        for d in D3:
            g2_copy(t, d, False).wait_recv()
        for d in D3:
            go(g1_copy(t, d))
        go(gc_copy(t, 0))

    def stage7(t):
        for d in D3:
            g1_copy(t, d, False).wait_recv()
            go(gc_copy(t, d))

    for t in range(4):
        stage1(t)
    for t in range(4):
        stage2(t)
    stage3()
    flush()
    stage4()
    stage5()
    flush()
    for t in range(4):
        stage6(t)
    for t in range(4):
        stage7(t)
    for t in range(4):
        for d in range(4):
            gc_arrived(t, d).wait_recv()
    flush()


def finish(pos_in, lse_in, dz_in, head_in, pos_ref, lse_ref, dz_ref, head_ref, buf, sem):
    copies = [
        pltpu.make_async_copy(dz_in, dz_ref, sem.at[0]),
        pltpu.make_async_copy(pos_in, pos_ref, sem.at[1]),
        pltpu.make_async_copy(lse_in, lse_ref, sem.at[2]),
    ]
    for cp in copies:
        cp.start()
    for i in range(8):
        rows = slice(i * 256, (i + 1) * 256)
        buf[rows, :] = head_in[rows, :].astype(F32)
        cp = pltpu.make_async_copy(buf.at[rows, :], head_ref.at[rows, :], sem.at[3 + i])
        cp.start()
        copies.append(cp)
    for cp in copies:
        cp.wait()


def on_device(features, head_weight, pairs):
    vmem = pl.BlockSpec(memory_space=pltpu.VMEM)
    dma = pltpu.SemaphoreType.DMA
    pos, lse, dz, head = pl.pallas_call(
        kernel,
        out_shape=(
            pltpu.VMEM((1, ROWS), F32),
            pltpu.VMEM((1, ROWS), F32),
            pltpu.VMEM((ROWS, PROJ), F32),
            pltpu.VMEM((HID, PROJ), BF16),
        ),
        in_specs=[vmem] * 3,
        out_specs=(vmem,) * 4,
        scratch_shapes=[
            pltpu.VMEM((NZ, 4 * ROWS, PROJ), BF16),
            pltpu.VMEM((NZ, ROWS, 4 * ROWS), F32),
            pltpu.VMEM((ROWS, PROJ), F32),
            pltpu.VMEM((ROWS, 1), F32),
            pltpu.VMEM((ROWS, 1), jnp.int32),
            pltpu.VMEM((ROWS, 128), F32),
            pltpu.VMEM((ROWS, 128), F32),
            pltpu.VMEM((32, 1, ROWS), F32),
            pltpu.VMEM((ROWS, PROJ), F32),
            pltpu.VMEM((ROWS, HID // 2), BF16),
            pltpu.VMEM((HID // 2, 2 * ROWS), BF16),
            pltpu.VMEM((2, ROWS, PROJ), BF16),
            pltpu.VMEM((4, 4, 64, PROJ), F32),
            pltpu.VMEM((4, 4, 64, PROJ), BF16),
            pltpu.VMEM((4, 3, 64, PROJ), BF16),
            pltpu.VMEM((4, 4, 16, PROJ), F32),
            pltpu.VMEM((4, 3, 16, PROJ), F32),
            pltpu.VMEM((4, 16, PROJ), F32),
            pltpu.VMEM((7, 16, 256), F32),
            pltpu.SemaphoreType.REGULAR,
            dma((2, 4, 3)), dma((2, 4, 3)),
            dma((2, 4)), dma((2, 4)),
            dma((2, 5, 2)), dma((2, 5, 2)),
            dma((32,)), dma((32,)),
            dma((2,)), dma((2,)),
            dma((4, 3)), dma((4, 3)),
            dma((4, 3)), dma((4, 3)),
            dma((7,)), dma((7,)),
            dma((7,)), dma((7,)),
            dma((4, 3)), dma((4, 3)),
            dma((4, 3)), dma((4, 3)),
            dma((4, 4)), dma((4, 4)),
        ],
        compiler_params=pltpu.CompilerParams(
            collective_id=0, has_side_effects=True, vmem_limit_bytes=44 << 20
        ),
        name="ntxent",
    )(features[0], head_weight, pairs)
    inputs = [pltpu.with_memory_space_constraint(a, pltpu.VMEM) for a in (pos, lse, dz, head)]
    pos, lse, dz, head = pl.pallas_call(
        finish,
        out_shape=(
            jax.ShapeDtypeStruct((1, ROWS), F32),
            jax.ShapeDtypeStruct((1, ROWS), F32),
            jax.ShapeDtypeStruct((ROWS, PROJ), F32),
            jax.ShapeDtypeStruct((HID, PROJ), F32),
        ),
        in_specs=[vmem] * 4,
        out_specs=(pl.BlockSpec(memory_space=pl.ANY),) * 4,
        scratch_shapes=[pltpu.VMEM((HID, PROJ), F32), dma((11,))],
        compiler_params=pltpu.CompilerParams(vmem_limit_bytes=16 << 20),
        name="finish",
    )(*inputs)
    return pos, lse, dz[None], head


def solution(mesh):
    in_specs = (P("group", "blk", None), P(), P("group", "blk"))
    out_specs = (P("group", "blk"), P("group", "blk"), P("group", "blk", None), P())
    return jax.shard_map(
        on_device, mesh=mesh, in_specs=in_specs, out_specs=out_specs, check_vma=False
    )
```

time: 105 us -> 96.9 us (0.923)
  Pallas kernels: 98.3 us -> 92.6 us
  other arithmetic: 4.26 us -> 0 us
  local copies, waits for them, and re-layouts: 1.93 us -> 3.49 us
    pallas_call x1 -> x2, Pallas kernels: 98.3 us -> 92.6 us  [the longest x1 90.3 us: on_device(): pl.pallas_call(kernel, out_shape=(pltpu.VMEM((1, ROWS), F32), pltpu.VMEM(...]
    convert_element_type x1 -> x0, other arithmetic: 4.26 us -> none  [on_device(): return (pos, lse, dz[None], head.astype(F32))]
    unnamed x9 -> x6, local copies, waits for them, and re-layouts: 1.93 us -> 3.49 us
where the time goes in v2:
time: 96.9 us; the launch traced here: 96.7 us
  Pallas kernels  92.6 us (96%)
  local copies, waits for them, and re-layouts  3.49 us (4%)
    pallas_call x1, Pallas kernels, on_device(): pl.pallas_call(kernel, out_shape=(pltpu.VMEM((1, ROWS), F32), pltpu.VMEM(...  90.3 us
    unnamed x6, local copies, waits for them, and re-layouts  3.49 us
    pallas_call x1, Pallas kernels, on_device(): pl.pallas_call(finish, out_shape=(jax.ShapeDtypeStruct((1, ROWS), F32), j...  2.28 us

profile of v2, /device:TPU:1, one launch (start us, length us, event | category | flops | bytes accessed | tf_op | source)
XLA Modules:
  0.0 96.7 jit_solution(6441620689349757628)
XLA Ops:
  0.6 0.0 copy-start
  0.6 1.6 %copy-done = bf16[2048,512]{1,0:T(8,128)(2,1)S(1)} copy-done((bf16[2048,512]{1,0:T(8,128)(2,1)S(1)}, bf16[2048,512]{1,0:T(8,128)(2,1)}, u32[]{:S(2)}) %copy-start) | copy-done | bytes 2097176
  2.2 0.0 copy-start.1
  2.2 1.2 %copy-done.1 = bf16[1,256,2048]{2,1,0:T(8,128)(2,1)S(1)} copy-done((bf16[1,256,2048]{2,1,0:T(8,128)(2,1)S(1)}, bf16[1,256,2048]{2,1,0:T(8,128)(2,1)}, u32[]{:S(2)}) %copy-start.1) | copy-done | bytes 1048600
  3.4 0.0 copy-start.2
  3.5 0.7 copy-done.2
  4.1 90.3 %ntxent.1 = (f32[1,256]{1,0:T(1,128)S(1)}, f32[1,256]{1,0:T(1,128)S(1)}, f32[256,512]{1,0:T(8,128)S(1)}, bf16[2048,512]{1,0:T(8,128)(2,1)S(1)}) custom-call(bf16[256,2048]{1,0:T(8,128)(2,1)S(1)} %bitcast.2, bf16[2048,512]{1,0:T(8,128)(2,1)S(1)} %copy-done, s32[1,256]{1,0:T(1,128)S(1)} %copy-done.2), custom_call_target="tpu_custom_call" | custom-call | tf_op jit(solution)/shard_map/ntxent/pallas_call | solution.py:439
  94.5 2.3 %finish.1 = (f32[1,256]{1,0:T(1,128)}, f32[1,256]{1,0:T(1,128)}, f32[256,512]{1,0:T(8,128)}, f32[2048,512]{1,0:T(8,128)}) custom-call(f32[1,256]{1,0:T(1,128)S(1)} %get-tuple-element.12.pos_in, f32[1,256]{1,0:T(1,128)S(1)} %get-tuple-element.13.lse_in, f32[256,512]{1,0:T(8,128)S(1)} %get-tuple-element.14.dz_in, bf16[2048,512]{1,0:T(8,128)(2,1)S(1)} %get-tuple-element.15.head_in), custom_call_target="tpu_custom_call" | custom-call | tf_op jit(solution)/shard_map/finish/pallas_call | solution.py:489
Async XLA Ops:
  0.6 1.6 %copy-start = (bf16[2048,512]{1,0:T(8,128)(2,1)S(1)}, bf16[2048,512]{1,0:T(8,128)(2,1)}, u32[]{:S(2)}) copy-start(bf16[2048,512]{1,0:T(8,128)(2,1)} %w_ref.1) | copy-start | bytes 6291460
  2.2 1.2 %copy-start.1 = (bf16[1,256,2048]{2,1,0:T(8,128)(2,1)S(1)}, bf16[1,256,2048]{2,1,0:T(8,128)(2,1)}, u32[]{:S(2)}) copy-start(bf16[1,256,2048]{2,1,0:T(8,128)(2,1)} %param.3) | copy-start | bytes 3145732
  3.4 0.7 copy-start.2

commit v3 on v2

--- a/solution.py
+++ b/solution.py
@@ -16,18 +16,28 @@
 ROWS = 256
 NZ = 8
 NA = (176, 160)
+KCUTS = 4
 INV_TEMP = 10.0
 LOG2E = 1.4426950408889634
 
-LAST = (((0, 144), (144, 112)), ((128, 128), (0, 128)))
+LAST = (
+    (1, 0, 0, 64),
+    (0, 0, 64, 112),
+    (0, 0, 176, 80),
+    (1, 1, 0, 96),
+    (0, 1, 176, 80),
+    (1, 1, 96, 80),
+)
+LATE_Y = ((1, 0, 96), (1, 96, 64), (0, 0, 176))
 
 
 def kernel(
-    feat_ref, w_ref, pairs_ref,
+    feat_hbm, w_hbm, pairs_hbm,
     pos_ref, lse_ref, dz_ref, head_ref,
+    feat_ref, w_ref, pairs_ref, load_sem,
     ub_all, e_all, u_s, inv_s, pcol_s, den_s, pos_s, rden_all, acc_s,
     f_sib, f_t, dzb, pf, sb1, r1, qf, r2, zb, r3, in_sem,
-    z_send, z_recv, y_send, y_recv, c_send, c_recv, d_send, d_recv,
+    z_send, z_recv, l_send, l_recv, lc_send, lc_recv, ly_send, ly_recv, y_send, y_recv, c_send, c_recv, d_send, d_recv,
     x_send, x_recv, s1_send, s1_recv, s2_send, s2_recv, s3_send, s3_recv,
     g3_send, g3_recv, g2_send, g2_recv, g1_send, g1_recv, gc_send, gc_recv,
 ):
@@ -60,7 +70,23 @@
     for to in znext + (sib,) + ring:
         pl.semaphore_signal(barrier, inc=1, device_id=to, device_id_type=MESH)
 
-    zz = jnp.dot(feat_ref[...], w_ref[...], preferred_element_type=F32)
+    def kcut(k):
+        return slice(k * (HID // KCUTS), (k + 1) * (HID // KCUTS))
+
+    loads = []
+    for k in range(KCUTS):
+        loads.append(pltpu.make_async_copy(feat_hbm.at[:, kcut(k)], feat_ref.at[:, kcut(k)], load_sem.at[2 * k]))
+        loads.append(pltpu.make_async_copy(w_hbm.at[kcut(k), :], w_ref.at[kcut(k), :], load_sem.at[2 * k + 1]))
+    loads.append(pltpu.make_async_copy(pairs_hbm, pairs_ref, load_sem.at[2 * KCUTS]))
+    for cp in loads:
+        cp.start()
+
+    zz = jnp.zeros((ROWS, PROJ), F32)
+    for k in range(KCUTS):
+        for cp in loads[2 * k : 2 * k + 2]:
+            cp.wait()
+        zz += jnp.dot(feat_ref[:, kcut(k)], w_ref[kcut(k), :], preferred_element_type=F32)
+    loads[-1].wait()
     inv = lax.rsqrt(jnp.sum(zz * zz, axis=1, keepdims=True) + 1e-06)
     u = zz * inv
     inv_s[...] = inv
@@ -78,19 +104,42 @@
     def piece(zo, yl_, c_, off, n):
         return ub_all.at[zo, rows_of(yl_, c_, off, n), :]
 
-    def z_ref(dr, s, kind, zo):
-        if s == 3:
-            return piece(zo, 1 - yl if kind else yl, c, *LAST[kind][dr])
+    def z_ref(dr, kind, zo):
         na = NA[dr]
         return piece(zo, 1 - yl if kind == 2 else yl, c, *((na, ROWS - na) if kind else (0, na)))
 
     def z_copy(dr, s, kind):
-        ref = z_ref(dr, s, kind, origin(dr, s))
+        ref = z_ref(dr, kind, origin(dr, s))
         return copy(ref, ref, z_send.at[dr, s, kind], z_recv.at[dr, s, kind], znext[dr])
 
     def z_arrived(dr, s, kind):
-        ref = z_ref(dr, s, kind, origin(dr, s + 1))
+        ref = z_ref(dr, kind, origin(dr, s + 1))
         return copy(ref, ref, z_send.at[dr, s, kind], z_recv.at[dr, s, kind], znext[dr])
+
+    def last_ref(i, hops, c_):
+        dr, other, off, n = LAST[i]
+        return piece(origin(dr, hops), 1 - yl if other else yl, c_, off, n)
+
+    def last_copy(i):
+        ref = last_ref(i, 3, c)
+        return copy(ref, ref, l_send.at[i], l_recv.at[i], znext[LAST[i][0]])
+
+    def last_arrived(i):
+        ref = last_ref(i, 4, c)
+        return copy(ref, ref, l_send.at[i], l_recv.at[i], znext[LAST[i][0]])
+
+    def last_chip_copy(i):
+        ref = last_ref(i, 4, c)
+        return copy(ref, ref, lc_send.at[i], lc_recv.at[i], sib)
+
+    def last_chip_arrived(i):
+        ref = last_ref(i, 4, 1 - c)
+        return copy(ref, ref, lc_send.at[i], lc_recv.at[i], sib)
+
+    def late_y(i, mine_):
+        dr, off, n = LATE_Y[i]
+        ref = piece(origin(dr, 3), yl if mine_ else 1 - yl, c, off, n)
+        return copy(ref, ref, ly_send.at[i], ly_recv.at[i], ynb)
 
     def y_ref(dr, s, yl_):
         if s == 0:
@@ -106,8 +155,7 @@
         return copy(ref, ref, y_send.at[dr, s], y_recv.at[dr, s], ynb)
 
     def c_ref(dr, s, other, c_):
-        part = LAST[other][dr] if s == 4 else (0, ROWS)
-        return piece(origin(dr, s), 1 - yl if other else yl, c_, *part)
+        return piece(origin(dr, s), 1 - yl if other else yl, c_, 0, ROWS)
 
     def c_copy(dr, s, other):
         ref = c_ref(dr, s, other, c)
@@ -175,51 +223,81 @@
     xcp.wait_recv()
     f_t[:, ROWS:] = f_sib[...].T
 
+    def scores_pair(dr, s, other):
+        c_arrived(dr, s, other).wait_recv()
+
+        def body(k, carry):
+            scores(origin(dr, s), (1 - yl if other else yl) * 2 + k)
+            return carry
+
+        lax.fori_loop(0, 2, body, 0)
+
     for s in (1, 2, 3):
         last = s == 3
+        drs = (0,) if s == 1 else (0, 1)
         for dr in (0, 1):
             z_arrived(dr, s - 1, 0).wait_recv()
-            if not last:
+            if last:
+                go(last_copy(1 - dr))
+            else:
                 go(z_copy(dr, s, 0))
-            elif dr == 0:
-                go(z_copy(0, 3, 0))
-            go(y_copy(dr, s))
+                go(y_copy(dr, s))
+        if last:
+            for i in range(3):
+                go(late_y(i, True))
+        for dr in drs:
+            scores_pair(dr, s - 1, 0)
         for dr in (0, 1):
             z_arrived(dr, s - 1, 1).wait_recv()
             if not last:
                 go(z_copy(dr, s, 1))
-            elif dr == 1:
-                go(z_copy(1, 3, 0))
+            elif dr == 0:
+                go(last_copy(2))
             go(c_copy(dr, s, 0))
+        if s > 1:
+            for dr in (0, 1):
+                y_arrived(dr, s - 1).wait_recv()
+                go(c_copy(dr, s - 1, 1))
         for dr in (0, 1):
             z_arrived(dr, s - 1, 2).wait_recv()
             if not last:
                 go(z_copy(dr, s, 2))
-        for dr in (0, 1) if s > 1 else (0,):
-            for other in (0, 1):
-                c_arrived(dr, s - 1, other).wait_recv()
-            scores_of(origin(dr, s - 1))
-        for dr in (0, 1):
-            y_arrived(dr, s).wait_recv()
-            if last:
-                go(z_copy(dr, 3, 1))
-            go(c_copy(dr, s, 1))
+            elif dr == 0:
+                go(last_copy(4))
+        if last:
+            late_y(0, False).wait_recv()
+            go(last_copy(3))
+            scores_pair(0, 2, 1)
+            late_y(1, False).wait_recv()
+            go(last_copy(5))
+            go(c_copy(1, 3, 1))
+            scores_pair(1, 2, 1)
+        else:
+            for dr in drs:
+                scores_pair(dr, s - 1, 1)
     for dr in (0, 1):
-        for other in (0, 1):
-            c_arrived(dr, 3, other).wait_recv()
-        scores_of(origin(dr, 3))
-    flush()
-    pl.semaphore_wait(in_sem, 4)
+        scores_pair(dr, 3, 0)
+    for i in (0, 1, 2):
+        last_arrived(i).wait_recv()
+        go(last_chip_copy(i))
+    scores_pair(1, 3, 1)
+    late_y(2, False).wait_recv()
+    go(c_copy(0, 3, 1))
     far = origin(0, 4)
-    for other in (0, 1):
-        for dr in (0, 1):
-            z_arrived(dr, 3, other).wait_recv()
-            go(c_copy(dr, 4, other))
-        scores(far, (1 - yl if other else yl) * 2 + c)
-    for other in (0, 1):
-        for dr in (0, 1):
-            c_arrived(dr, 4, other).wait_recv()
-        scores(far, (1 - yl if other else yl) * 2 + 1 - c)
+    scores(far, yl * 2 + c)
+    for i in (3, 4):
+        last_arrived(i).wait_recv()
+        go(last_chip_copy(i))
+    scores_pair(0, 3, 1)
+    last_arrived(5).wait_recv()
+    go(last_chip_copy(5))
+    scores(far, (1 - yl) * 2 + c)
+    for i in (0, 1, 2):
+        last_chip_arrived(i).wait_recv()
+    scores(far, yl * 2 + 1 - c)
+    for i in (3, 4, 5):
+        last_chip_arrived(i).wait_recv()
+    scores(far, (1 - yl) * 2 + 1 - c)
 
     den = jnp.sum(den_s[...], axis=1, keepdims=True)
     r_own = 1.0 / den
@@ -247,6 +325,7 @@
             if dz_ or k:
                 go(d_copy(dz_, k))
 
+    pl.semaphore_wait(in_sem, 4)
     lse_ref[...] = jnp.broadcast_to(jnp.log(den), (ROWS, 128)).T[:1, :]
     pos = jnp.sum(pos_s[...], axis=1, keepdims=True) * INV_TEMP
     pos_ref[...] = jnp.broadcast_to(pos, (ROWS, 128)).T[:1, :]
@@ -444,9 +523,13 @@
             pltpu.VMEM((ROWS, PROJ), F32),
             pltpu.VMEM((HID, PROJ), BF16),
         ),
-        in_specs=[vmem] * 3,
+        in_specs=[pl.BlockSpec(memory_space=pltpu.HBM)] * 3,
         out_specs=(vmem,) * 4,
         scratch_shapes=[
+            pltpu.VMEM((ROWS, HID), BF16),
+            pltpu.VMEM((HID, PROJ), BF16),
+            pltpu.VMEM((1, ROWS), jnp.int32),
+            dma((2 * KCUTS + 1,)),
             pltpu.VMEM((NZ, 4 * ROWS, PROJ), BF16),
             pltpu.VMEM((NZ, ROWS, 4 * ROWS), F32),
             pltpu.VMEM((ROWS, PROJ), F32),
@@ -467,9 +550,12 @@
             pltpu.VMEM((4, 16, PROJ), F32),
             pltpu.VMEM((7, 16, 256), F32),
             pltpu.SemaphoreType.REGULAR,
-            dma((2, 4, 3)), dma((2, 4, 3)),
-            dma((2, 4)), dma((2, 4)),
-            dma((2, 5, 2)), dma((2, 5, 2)),
+            dma((2, 3, 3)), dma((2, 3, 3)),
+            dma((6,)), dma((6,)),
+            dma((6,)), dma((6,)),
+            dma((3,)), dma((3,)),
+            dma((2, 3)), dma((2, 3)),
+            dma((2, 4, 2)), dma((2, 4, 2)),
             dma((32,)), dma((32,)),
             dma((2,)), dma((2,)),
             dma((4, 3)), dma((4, 3)),
@@ -484,7 +570,7 @@
             collective_id=0, has_side_effects=True, vmem_limit_bytes=44 << 20
         ),
         name="ntxent",
-    )(features[0], head_weight, pairs)
+    )(*[pltpu.with_memory_space_constraint(a, pltpu.HBM) for a in (features[0], head_weight, pairs)])
     inputs = [pltpu.with_memory_space_constraint(a, pltpu.VMEM) for a in (pos, lse, dz, head)]
     pos, lse, dz, head = pl.pallas_call(
         finish,

time: 96.9 us -> 92.5 us (0.955)
  local copies, waits for them, and re-layouts: 3.49 us -> 0 us
    unnamed x6 -> x0, local copies, waits for them, and re-layouts: 3.49 us -> none
where the time goes in v3:
time: 92.5 us; the launch traced here: 92.4 us
  Pallas kernels  91.8 us (99%)
    pallas_call x1, Pallas kernels, on_device(): pl.pallas_call(kernel, out_shape=(pltpu.VMEM((1, ROWS), F32), pltpu.VMEM(...  89.5 us
    pallas_call x1, Pallas kernels, on_device(): pl.pallas_call(finish, out_shape=(jax.ShapeDtypeStruct((1, ROWS), F32), j...  2.28 us

profile of v3, /device:TPU:1, one launch (start us, length us, event | category | flops | bytes accessed | tf_op | source)
XLA Modules:
  0.0 92.4 jit_solution(2352272993244730505)
XLA Ops:
  0.6 89.5 %ntxent.1 = (f32[1,256]{1,0:T(1,128)S(1)}, f32[1,256]{1,0:T(1,128)S(1)}, f32[256,512]{1,0:T(8,128)S(1)}, bf16[2048,512]{1,0:T(8,128)(2,1)S(1)}) custom-call(bf16[256,2048]{1,0:T(8,128)(2,1)} %bitcast.2, bf16[2048,512]{1,0:T(8,128)(2,1)} %w_hbm.1, s32[1,256]{1,0:T(1,128)} %pairs_hbm.1), custom_call_target="tpu_custom_call" | custom-call | tf_op jit(solution)/shard_map/ntxent/pallas_call | solution.py:518
  90.1 2.3 %finish.1 = (f32[1,256]{1,0:T(1,128)}, f32[1,256]{1,0:T(1,128)}, f32[256,512]{1,0:T(8,128)}, f32[2048,512]{1,0:T(8,128)}) custom-call(f32[1,256]{1,0:T(1,128)S(1)} %get-tuple-element.12.pos_in, f32[1,256]{1,0:T(1,128)S(1)} %get-tuple-element.13.lse_in, f32[256,512]{1,0:T(8,128)S(1)} %get-tuple-element.14.dz_in, bf16[2048,512]{1,0:T(8,128)(2,1)S(1)} %get-tuple-element.15.head_in), custom_call_target="tpu_custom_call" | custom-call | tf_op jit(solution)/shard_map/finish/pallas_call | solution.py:575

commit v4 on v2

v4 whole, which is shorter than its diff:
```python
import functools

import jax
import jax.numpy as jnp
from jax import lax
from jax.experimental import pallas as pl
from jax.experimental.pallas import tpu as pltpu
from jax.sharding import PartitionSpec as P

MESH = pl.DeviceIdType.MESH
F32 = jnp.float32
BF16 = jnp.bfloat16

HID = 2048
PROJ = 512
ROWS = 256
NZ = 8
LOW = True
CUT = 64
KCUTS = 4
INV_TEMP = 10.0
LOG2E = 1.4426950408889634


def kernel(
    feat_hbm, w_hbm, pairs_hbm,
    pos_ref, lse_ref, dz_ref, head_ref,
    feat_ref, w_ref, pairs_ref, load_sem,
    ub_all, ub_r, e_all, u_s, inv_s, pcol_s, den_s, pos_s, den_mine, den_all, den_o, pos_x, pos_y,
    acc_s, feat_o, pairs_o, f_sib, f_t, dzh, dzl, dzx, pf, sb1, r1, qf, r2, zb, r3, in_sem,
    z_send, z_recv, y_send, y_recv, fy_send, fy_recv, c_send, c_recv, fc_send, fc_recv,
    d_send, d_recv, x_send, x_recv, s1_send, s1_recv, s2_send, s2_recv, s3_send, s3_recv,
    g3_send, g3_recv, g2_send, g2_recv, g1_send, g1_recv, gc_send, gc_recv,
):
    blk = lax.axis_index("blk")
    grp = lax.axis_index("group")
    z, yl, c = blk // 4, lax.rem(blk // 2, 2), lax.rem(blk, 2)
    yh, x = grp // 4, lax.rem(grp, 4)
    y = yh * 2 + yl

    def dev(z_, y_, c_, x_):
        return ((z_ * 2 + lax.rem(y_, 2)) * 2 + c_, (y_ // 2) * 4 + x_)

    def copy(src, dst, ssem, rsem, to):
        return pltpu.make_async_remote_copy(
            src_ref=src, dst_ref=dst, send_sem=ssem, recv_sem=rsem,
            device_id=to, device_id_type=MESH,
        )

    sib = dev(z, y, 1 - c, x)
    ynb = (blk + 2 - 4 * yl, grp)

    barrier = pltpu.get_barrier_semaphore()
    ring = (
        dev(z, y, c, lax.rem(x + 1, 4)),
        dev(z, y, c, lax.rem(x + 3, 4)),
        dev(z, lax.rem(y + 1, 4), c, x),
        dev(z, lax.rem(y + 3, 4), c, x),
    )
    znext = (dev(lax.rem(z + 1, NZ), y, c, x), dev(lax.rem(z + NZ - 1, NZ), y, c, x))
    for to in znext + (sib,) + ring:
        pl.semaphore_signal(barrier, inc=1, device_id=to, device_id_type=MESH)

    def kcut(k):
        return slice(k * (HID // KCUTS), (k + 1) * (HID // KCUTS))

    loads = []
    for k in range(KCUTS):
        loads.append(pltpu.make_async_copy(feat_hbm.at[:, kcut(k)], feat_ref.at[:, kcut(k)], load_sem.at[2 * k]))
        loads.append(pltpu.make_async_copy(w_hbm.at[kcut(k), :], w_ref.at[kcut(k), :], load_sem.at[2 * k + 1]))
    loads.append(pltpu.make_async_copy(pairs_hbm, pairs_ref, load_sem.at[2 * KCUTS]))
    for cp in loads:
        cp.start()

    zz = jnp.zeros((ROWS, PROJ), F32)
    for k in range(KCUTS):
        for cp in loads[2 * k : 2 * k + 2]:
            cp.wait()
        zz += jnp.dot(feat_ref[:, kcut(k)], w_ref[kcut(k), :], preferred_element_type=F32)
    loads[-1].wait()
    inv = lax.rsqrt(jnp.sum(zz * zz, axis=1, keepdims=True) + 1e-06)
    u = zz * inv
    inv_s[:ROWS] = inv
    u_s[:ROWS] = u
    ub = u.astype(BF16)
    ub_r[0] = ub
    ub_all[z, pl.ds(pl.multiple_of(c * ROWS, ROWS), ROWS), :] = ub
    pl.semaphore_wait(barrier, 7)

    def origin(dr, s):
        return lax.rem(z + NZ + (-s if dr == 0 else s), NZ)

    def piece(zo, c_, off, n):
        return ub_all.at[zo, pl.ds(pl.multiple_of(c_ * ROWS + off, 16), n), :]

    def z_copy(dr, s, p):
        ref = piece(origin(dr, s), c, p * CUT, CUT)
        return copy(ref, ref, z_send.at[dr, s, p], z_recv.at[dr, s, p], znext[dr])

    def z_arrived(dr, s, p):
        ref = piece(origin(dr, s + 1), c, p * CUT, CUT)
        return copy(ref, ref, z_send.at[dr, s, p], z_recv.at[dr, s, p], znext[dr])

    def c_ref(dr, s, c_):
        return piece(origin(dr, s), c_, *((dr * 128, 128) if s == 4 else (0, ROWS)))

    def c_copy(dr, s):
        ref = c_ref(dr, s, c)
        return copy(ref, ref, c_send.at[dr, s], c_recv.at[dr, s], sib)

    def c_arrived(dr, s):
        ref = c_ref(dr, s, 1 - c)
        return copy(ref, ref, c_send.at[dr, s], c_recv.at[dr, s], sib)

    sent = []

    def go(cp):
        cp.start()
        sent.append(cp)

    def flush():
        for cp in sent:
            cp.wait_send()
        sent.clear()

    yub = copy(ub_r.at[0], ub_r.at[1], y_send.at[0], y_recv.at[0], ynb)
    ypairs = copy(pairs_ref, pairs_o, y_send.at[1], y_recv.at[1], ynb)
    go(yub)
    go(ypairs)
    for p in range(4):
        for dr in (0, 1):
            go(z_copy(dr, 0, p))
    go(c_copy(0, 0))

    def fy_copy(k):
        return copy(feat_ref.at[:, kcut(k)], feat_o.at[:, kcut(k)], fy_send.at[k], fy_recv.at[k], ynb)

    for k in range(KCUTS):
        go(fy_copy(k))
    for to in ring:
        pl.semaphore_signal(in_sem, inc=1, device_id=to, device_id_type=MESH)

    half = HID // 2
    cut = HID // KCUTS
    mine = pl.multiple_of(c * half, half)
    theirs = pl.multiple_of((1 - c) * half, half)
    xcp = copy(feat_ref.at[:, pl.ds(theirs, half)], f_sib.at[0], x_send.at[0], x_recv.at[0], sib)
    go(xcp)

    def fc_copy(q):
        cols = pl.ds(pl.multiple_of((1 - c) * half + q * cut, cut), cut)
        dst = f_sib.at[1, :, q * cut : (q + 1) * cut]
        return copy(feat_o.at[:, cols], dst, fc_send.at[q], fc_recv.at[q], sib)

    den_s[...] = jnp.zeros_like(den_s)
    pos_s[...] = jnp.zeros_like(pos_s)
    sub = lax.broadcasted_iota(jnp.int32, (2 * ROWS, 1), 0)
    other_blk = blk + 2 - 4 * yl
    own_row = jnp.where(sub < ROWS, blk * ROWS, other_blk * ROWS - ROWS) + sub

    def column(row):
        return jnp.broadcast_to(row, (128, ROWS)).T[:, :1]

    def cols_of(zo, k):
        first = (zo * 4 + yl * 2 + k) * ROWS
        return first + lax.broadcasted_iota(jnp.int32, (2 * ROWS, ROWS), 1)

    def scores(zo, k):
        lanes = pl.ds(pl.multiple_of(k * ROWS, ROWS), ROWS)
        s = lax.dot_general(
            ub_r[...].reshape(2 * ROWS, PROJ), ub_all[zo, lanes, :],
            (((1,), (1,)), ((), ())), preferred_element_type=F32,
        )
        cols = cols_of(zo, k)
        e = jnp.where(cols == own_row, 0.0, jnp.exp2(s * (INV_TEMP * LOG2E)))
        e_all[zo, :, lanes] = e
        p = jnp.where(cols == pcol_s[...], s, 0.0)
        den_s[...] += e[:, :128] + e[:, 128:]
        pos_s[...] += p[:, :128] + p[:, 128:]

    def other_z(k):
        fy_copy(k).wait_recv()
        part = jnp.dot(feat_o[:, kcut(k)], w_ref[kcut(k), :], preferred_element_type=F32)
        if k == 0:
            u_s[ROWS:] = part
        else:
            u_s[ROWS:] += part

    for s in (1, 2, 3):
        for p in range(4):
            for dr in (0, 1):
                z_arrived(dr, s - 1, p).wait_recv()
                if s < 3 or p // 2 == dr:
                    go(z_copy(dr, s, p))
                if p == 3:
                    go(c_copy(dr, s))
            if s == 1:
                if p == 1:
                    f_t[:, :ROWS] = feat_ref[:, pl.ds(mine, half)].T
                if p == 2:
                    xcp.wait_recv()
                    f_t[:, 2 * ROWS : 3 * ROWS] = f_sib[0].T
                if p == 3:
                    yub.wait_recv()
                    ypairs.wait_recv()
                    pcol_s[:ROWS] = column(pairs_ref[...])
                    pcol_s[ROWS:] = column(pairs_o[...])
                    scores(z, c)
                    c_arrived(0, 0).wait_recv()
                    scores(z, 1 - c)
            else:
                dr = p % 2
                if p >= 2:
                    c_arrived(dr, s - 1).wait_recv()
                scores(origin(dr, s - 1), c if p < 2 else 1 - c)
    for dr in (0, 1):
        scores(origin(dr, 3), c)
    other_z(0)
    for dr in (0, 1):
        c_arrived(dr, 3).wait_recv()
        scores(origin(dr, 3), 1 - c)
    far = origin(0, 4)
    for dr in (0, 1):
        for p in (2 * dr, 2 * dr + 1):
            z_arrived(dr, 3, p).wait_recv()
        go(c_copy(dr, 4))
    scores(far, c)
    for dr in (0, 1):
        c_arrived(dr, 4).wait_recv()
    scores(far, 1 - c)

    sums = jnp.broadcast_to(jnp.sum(den_s[...], axis=1, keepdims=True), (2 * ROWS, 128)).T
    den_mine[0] = sums[:1, :ROWS]
    den_mine[1] = sums[:1, ROWS:]
    den_all[0, z * 2 + c] = sums[:1, :ROWS]

    def d_copy(dz_, dy, dc):
        to_blk = lax.rem(z + dz_, NZ) * 4 + lax.rem(yl + dy, 2) * 2 + lax.rem(c + dc, 2)
        i = dz_ * 4 + dy * 2 + dc
        return copy(
            den_mine.at[dy], den_all.at[dy, z * 2 + c], d_send.at[i], d_recv.at[i], (to_blk, grp)
        )

    def d_arrived(dz_, dy, dc):
        i = dz_ * 4 + dy * 2 + dc
        ref = den_all.at[dy, lax.rem(z + NZ - dz_, NZ) * 2 + lax.rem(c + dc, 2)]
        return copy(ref, ref, d_send.at[i], d_recv.at[i], (blk, grp))

    docp = copy(den_mine.at[0], den_o, y_send.at[2], y_recv.at[2], ynb)
    for dz_ in (4, 3, 5, 2, 6, 1, 7, 0):
        if dz_ == 2:
            go(docp)
            go(d_copy(0, 1, 0))
        for dy in (0, 1):
            for dc in (0, 1):
                if dz_ or dc:
                    go(d_copy(dz_, dy, dc))

    psum = jnp.broadcast_to(jnp.sum(pos_s[...], axis=1, keepdims=True), (2 * ROWS, 128)).T
    pos_y[...] = psum[:1, ROWS:]
    pcp = copy(pos_y, pos_x, y_send.at[3], y_recv.at[3], ynb)
    go(pcp)
    pos_ref[...] = psum[:1, :ROWS]
    other_z(1)

    docp.wait_recv()
    d_arrived(0, 1, 0).wait_recv()
    me2 = z * 2 + c
    den_own = den_all[0, me2] + den_all[1, me2]
    lse_ref[...] = jnp.log(den_own)
    r_rows = 1.0 / jnp.concatenate([column(den_own), column(den_o[...] + den_mine[1])], axis=0)
    for n, dz_ in enumerate((0, 1, 7, 2, 6, 3, 5, 4)):
        for dy in (0, 1):
            for dc in (0, 1):
                if dz_ or dc:
                    d_arrived(dz_, dy, dc).wait_recv()
        zo = lax.rem(z + NZ - dz_, NZ)
        parts = []
        for k in range(2):
            r_cols = 1.0 / (den_all[0, zo * 2 + k] + den_all[1, zo * 2 + k])
            e = e_all[zo, :, k * ROWS : (k + 1) * ROWS]
            h = e * (r_rows + r_cols) - jnp.where(cols_of(zo, k) == pcol_s[...], 2.0, 0.0)
            parts.append(h.astype(BF16))
        g = jnp.dot(
            jnp.concatenate(parts, axis=1), ub_all[zo], preferred_element_type=F32
        )
        if n == 0:
            acc_s[...] = g
        else:
            acc_s[...] += g

    def other_half(q):
        cols = pl.ds(pl.multiple_of(c * half + q * cut, cut), cut)
        f_t[q * cut : (q + 1) * cut, ROWS : 2 * ROWS] = feat_o[:, cols].T

    other_z(2)
    other_z(3)
    for q in (0, 1):
        go(fc_copy(q))
    zo_ = u_s[ROWS:]
    inv_o = lax.rsqrt(jnp.sum(zo_ * zo_, axis=1, keepdims=True) + 1e-06)
    u_s[ROWS:] = zo_ * inv_o
    inv_s[ROWS:] = inv_o

    slope = acc_s[...] * INV_TEMP
    u = u_s[...]
    dz = inv_s[...] * (slope - u * jnp.sum(u * slope, axis=1, keepdims=True))
    dz_ref[...] = dz[:ROWS]
    hi = dz.astype(BF16)
    dzh[:2] = hi.reshape(2, ROWS, PROJ)
    xcp = copy(dzh.at[pl.ds(0, 2)], dzh.at[pl.ds(2, 2)], x_send.at[1], x_recv.at[1], sib)
    go(xcp)
    if LOW:
        dzl[:2] = (dz - hi.astype(F32)).astype(BF16).reshape(2, ROWS, PROJ)
        lcp = copy(dzl.at[pl.ds(0, 2)], dzl.at[pl.ds(2, 2)], x_send.at[2], x_recv.at[2], sib)
        go(lcp)
    for q in (0, 1):
        other_half(q)
        fc_copy(q).wait_recv()
        f_t[q * cut : (q + 1) * cut, 3 * ROWS :] = f_sib[1, :, q * cut : (q + 1) * cut].T
    xcp.wait_recv()
    if LOW:
        lcp.wait_recv()
    pl.semaphore_wait(in_sem, 4)
    ycp = copy(dzh.at[1], dzx, y_send.at[4], y_recv.at[4], ynb)

    def along(t, first, d):
        if (t % 2 == 0) == first:
            return dev(z, y, c, lax.rem(x + d, 4))
        return dev(z, lax.rem(y + d, 4), c, x)

    def place(t, first):
        return x if (t % 2 == 0) == first else y

    def s1_copy(t, d):
        j = lax.rem(place(t, True) + d, 4)
        return copy(sb1.at[t, j], r1.at[t, d - 1], s1_send.at[t, d - 1], s1_recv.at[t, d - 1], along(t, True, d))

    def s2_copy(t, d):
        j = lax.rem(place(t, False) + d, 4)
        return copy(qf.at[t, j], r2.at[t, d - 1], s2_send.at[t, d - 1], s2_recv.at[t, d - 1], along(t, False, d))

    def out_rows(t, a, b, n):
        start = c * (HID // 2) + t * 256 + a * 64 + b * 16
        return pl.ds(pl.multiple_of(start, 16), n)

    def zcols(j):
        return pl.ds(pl.multiple_of(lax.rem(j, 2) * 256, 256), 256)

    def zpeer(d):
        return dev(lax.rem(z + d, NZ), y, c, x)

    def s3_copy(d):
        j = lax.rem(z + d, NZ)
        return copy(zb.at[j // 2, :, zcols(j)], r3.at[d - 1], s3_send.at[d - 1], s3_recv.at[d - 1], zpeer(d))

    def zrows(j):
        t = j // 2
        odd = lax.rem(t, 2)
        return out_rows(t, x + odd * (y - x), y + odd * (x - y), 16)

    def g3_copy(d, mine_=True):
        j = z if mine_ else lax.rem(z + NZ - d, NZ)
        ref = head_ref.at[zrows(j), zcols(j)]
        return copy(ref, ref, g3_send.at[d - 1], g3_recv.at[d - 1], zpeer(d))

    def g2_copy(t, d, mine_=True):
        b = place(t, False)
        ref = head_ref.at[out_rows(t, place(t, True), b if mine_ else lax.rem(b + 4 - d, 4), 16), :]
        return copy(ref, ref, g2_send.at[t, d - 1], g2_recv.at[t, d - 1], along(t, False, d))

    def g1_copy(t, d, mine_=True):
        a = place(t, True)
        ref = head_ref.at[out_rows(t, a if mine_ else lax.rem(a + 4 - d, 4), 0, 64), :]
        return copy(ref, ref, g1_send.at[t, d - 1], g1_recv.at[t, d - 1], along(t, True, d))

    def gc_copy(t, d):
        a = place(t, True)
        ref = head_ref.at[out_rows(t, lax.rem(a + 4 - d, 4), 0, 64), :]
        return copy(ref, ref, gc_send.at[t, d], gc_recv.at[t, d], sib)

    def gc_arrived(t, d):
        start = (1 - c) * (HID // 2) + t * 256 + lax.rem(place(t, True) + 4 - d, 4) * 64
        ref = head_ref.at[pl.ds(pl.multiple_of(start, 64), 64), :]
        return copy(ref, ref, gc_send.at[t, d], gc_recv.at[t, d], sib)

    D3, D7 = (2, 1, 3), (4, 3, 5, 2, 6, 1, 7)

    def stage1(t):
        ft = f_t[t * 256 : (t + 1) * 256, :]
        part = jnp.dot(ft, dzh[...].reshape(4 * ROWS, PROJ), preferred_element_type=F32)
        if LOW:
            part += jnp.dot(ft, dzl[...].reshape(4 * ROWS, PROJ), preferred_element_type=F32)
        pf[t] = part.reshape(4, 64, PROJ)
        sb1[t] = part.astype(BF16).reshape(4, 64, PROJ)
        for d in D3:
            go(s1_copy(t, d))

    def stage2(t):
        for d in D3:
            s1_copy(t, d).wait_recv()
        total = pf[t, place(t, True)]
        for d in range(3):
            total = total + r1[t, d].astype(F32)
        qf[t] = total.reshape(4, 16, PROJ)
        for d in D3:
            go(s2_copy(t, d))

    def stage3():
        for t in range(4):
            for d in D3:
                s2_copy(t, d).wait_recv()
            zb[t] = qf[t, place(t, False)] + r2[t, 0] + r2[t, 1] + r2[t, 2]
        for d in D7:
            go(s3_copy(d))

    def stage4():
        total = zb[z // 2, :, zcols(z)]
        for d in D7:
            s3_copy(d).wait_recv()
        for d in range(7):
            total = total + r3[d]
        head_ref[zrows(z), zcols(z)] = total.astype(BF16)
        for d in D7:
            go(g3_copy(d))

    def stage5():
        for d in D7:
            g3_copy(d, False).wait_recv()
        for t in range(4):
            for d in D3:
                go(g2_copy(t, d))

    def stage6(t):
        for d in D3:
            g2_copy(t, d, False).wait_recv()
        for d in D3:
            go(g1_copy(t, d))
        go(gc_copy(t, 0))

    def stage7(t):
        for d in D3:
            g1_copy(t, d, False).wait_recv()
            go(gc_copy(t, d))

    for t in range(4):
        stage1(t)
    for t in range(4):
        stage2(t)
    stage3()
    go(ycp)
    flush()
    stage4()
    stage5()
    flush()
    for t in range(4):
        stage6(t)
    ycp.wait_recv()
    dz_ref[...] += dzx[...].astype(F32)
    pcp.wait_recv()
    pos_ref[...] = (pos_ref[...] + pos_x[...]) * INV_TEMP
    for t in range(4):
        stage7(t)
    for t in range(4):
        for d in range(4):
            gc_arrived(t, d).wait_recv()
    flush()


def finish(pos_in, lse_in, dz_in, head_in, pos_ref, lse_ref, dz_ref, head_ref, buf, sem):
    copies = [
        pltpu.make_async_copy(dz_in, dz_ref, sem.at[0]),
        pltpu.make_async_copy(pos_in, pos_ref, sem.at[1]),
        pltpu.make_async_copy(lse_in, lse_ref, sem.at[2]),
    ]
    for cp in copies:
        cp.start()
    for i in range(8):
        rows = slice(i * 256, (i + 1) * 256)
        buf[rows, :] = head_in[rows, :].astype(F32)
        cp = pltpu.make_async_copy(buf.at[rows, :], head_ref.at[rows, :], sem.at[3 + i])
        cp.start()
        copies.append(cp)
    for cp in copies:
        cp.wait()


def on_device(features, head_weight, pairs):
    vmem = pl.BlockSpec(memory_space=pltpu.VMEM)
    dma = pltpu.SemaphoreType.DMA
    pos, lse, dz, head = pl.pallas_call(
        kernel,
        out_shape=(
            pltpu.VMEM((1, ROWS), F32),
            pltpu.VMEM((1, ROWS), F32),
            pltpu.VMEM((ROWS, PROJ), F32),
            pltpu.VMEM((HID, PROJ), BF16),
        ),
        in_specs=[pl.BlockSpec(memory_space=pltpu.HBM)] * 3,
        out_specs=(vmem,) * 4,
        scratch_shapes=[
            pltpu.VMEM((ROWS, HID), BF16),
            pltpu.VMEM((HID, PROJ), BF16),
            pltpu.VMEM((1, ROWS), jnp.int32),
            dma((2 * KCUTS + 1,)),
            pltpu.VMEM((NZ, 2 * ROWS, PROJ), BF16),
            pltpu.VMEM((2, ROWS, PROJ), BF16),
            pltpu.VMEM((NZ, 2 * ROWS, 2 * ROWS), F32),
            pltpu.VMEM((2 * ROWS, PROJ), F32),
            pltpu.VMEM((2 * ROWS, 1), F32),
            pltpu.VMEM((2 * ROWS, 1), jnp.int32),
            pltpu.VMEM((2 * ROWS, 128), F32),
            pltpu.VMEM((2 * ROWS, 128), F32),
            pltpu.VMEM((2, 1, ROWS), F32),
            pltpu.VMEM((2, 2 * NZ, 1, ROWS), F32),
            pltpu.VMEM((1, ROWS), F32),
            pltpu.VMEM((1, ROWS), F32),
            pltpu.VMEM((1, ROWS), F32),
            pltpu.VMEM((2 * ROWS, PROJ), F32),
            pltpu.VMEM((ROWS, HID), BF16),
            pltpu.VMEM((1, ROWS), jnp.int32),
            pltpu.VMEM((2, ROWS, HID // 2), BF16),
            pltpu.VMEM((HID // 2, 4 * ROWS), BF16),
            pltpu.VMEM((4, ROWS, PROJ), BF16),
            pltpu.VMEM((4, ROWS, PROJ), BF16),
            pltpu.VMEM((ROWS, PROJ), BF16),
            pltpu.VMEM((4, 4, 64, PROJ), F32),
            pltpu.VMEM((4, 4, 64, PROJ), BF16),
            pltpu.VMEM((4, 3, 64, PROJ), BF16),
            pltpu.VMEM((4, 4, 16, PROJ), F32),
            pltpu.VMEM((4, 3, 16, PROJ), F32),
            pltpu.VMEM((4, 16, PROJ), F32),
            pltpu.VMEM((7, 16, 256), F32),
            pltpu.SemaphoreType.REGULAR,
            dma((2, 4, 4)), dma((2, 4, 4)),
            dma((5,)), dma((5,)),
            dma((KCUTS,)), dma((KCUTS,)),
            dma((2, 5)), dma((2, 5)),
            dma((2,)), dma((2,)),
            dma((32,)), dma((32,)),
            dma((3,)), dma((3,)),
            dma((4, 3)), dma((4, 3)),
            dma((4, 3)), dma((4, 3)),
            dma((7,)), dma((7,)),
            dma((7,)), dma((7,)),
            dma((4, 3)), dma((4, 3)),
            dma((4, 3)), dma((4, 3)),
            dma((4, 4)), dma((4, 4)),
        ],
        compiler_params=pltpu.CompilerParams(
            collective_id=0, has_side_effects=True, vmem_limit_bytes=44 << 20
        ),
        name="ntxent",
    )(*[pltpu.with_memory_space_constraint(a, pltpu.HBM) for a in (features[0], head_weight, pairs)])
    inputs = [pltpu.with_memory_space_constraint(a, pltpu.VMEM) for a in (pos, lse, dz, head)]
    pos, lse, dz, head = pl.pallas_call(
        finish,
        out_shape=(
            jax.ShapeDtypeStruct((1, ROWS), F32),
            jax.ShapeDtypeStruct((1, ROWS), F32),
            jax.ShapeDtypeStruct((ROWS, PROJ), F32),
            jax.ShapeDtypeStruct((HID, PROJ), F32),
        ),
        in_specs=[vmem] * 4,
        out_specs=(pl.BlockSpec(memory_space=pl.ANY),) * 4,
        scratch_shapes=[pltpu.VMEM((HID, PROJ), F32), dma((11,))],
        compiler_params=pltpu.CompilerParams(vmem_limit_bytes=16 << 20),
        name="finish",
    )(*inputs)
    return pos, lse, dz[None], head


def solution(mesh):
    in_specs = (P("group", "blk", None), P(), P("group", "blk"))
    out_specs = (P("group", "blk"), P("group", "blk"), P("group", "blk", None), P())
    return jax.shard_map(
        on_device, mesh=mesh, in_specs=in_specs, out_specs=out_specs, check_vma=False
    )
```

time: 96.9 us -> 88.8 us (0.916)
  Pallas kernels: 92.6 us -> 88.1 us
  local copies, waits for them, and re-layouts: 3.49 us -> 0 us
    pallas_call x1, Pallas kernels: 90.3 us -> 85.8 us  [on_device(): pl.pallas_call(kernel, out_shape=(pltpu.VMEM((1, ROWS), F32), pltpu.VMEM(...]
    unnamed x6 -> x0, local copies, waits for them, and re-layouts: 3.49 us -> none
where the time goes in v4:
time: 88.8 us; the launch traced here: 88.7 us
  Pallas kernels  88.1 us (99%)
    pallas_call x1, Pallas kernels, on_device(): pl.pallas_call(kernel, out_shape=(pltpu.VMEM((1, ROWS), F32), pltpu.VMEM(...  85.8 us
    pallas_call x1, Pallas kernels, on_device(): pl.pallas_call(finish, out_shape=(jax.ShapeDtypeStruct((1, ROWS), F32), j...  2.28 us

profile of v4, /device:TPU:1, one launch (start us, length us, event | category | flops | bytes accessed | tf_op | source)
XLA Modules:
  0.0 88.7 jit_solution(15137304104928449766)
XLA Ops:
  0.6 85.8 %ntxent.1 = (f32[1,256]{1,0:T(1,128)S(1)}, f32[1,256]{1,0:T(1,128)S(1)}, f32[256,512]{1,0:T(8,128)S(1)}, bf16[2048,512]{1,0:T(8,128)(2,1)S(1)}) custom-call(bf16[256,2048]{1,0:T(8,128)(2,1)} %bitcast.2, bf16[2048,512]{1,0:T(8,128)(2,1)} %w_hbm.1, s32[1,256]{1,0:T(1,128)} %pairs_hbm.1), custom_call_target="tpu_custom_call" | custom-call | tf_op jit(solution)/shard_map/ntxent/pallas_call | solution.py:491
  86.5 2.3 %finish.1 = (f32[1,256]{1,0:T(1,128)}, f32[1,256]{1,0:T(1,128)}, f32[256,512]{1,0:T(8,128)}, f32[2048,512]{1,0:T(8,128)}) custom-call(f32[1,256]{1,0:T(1,128)S(1)} %get-tuple-element.12.pos_in, f32[1,256]{1,0:T(1,128)S(1)} %get-tuple-element.13.lse_in, f32[256,512]{1,0:T(8,128)S(1)} %get-tuple-element.14.dz_in, bf16[2048,512]{1,0:T(8,128)(2,1)S(1)} %get-tuple-element.15.head_in), custom_call_target="tpu_custom_call" | custom-call | tf_op jit(solution)/shard_map/finish/pallas_call | solution.py:556

commit v5 on v4

--- a/solution.py
+++ b/solution.py
@@ -15,7 +15,6 @@
 PROJ = 512
 ROWS = 256
 NZ = 8
-LOW = True
 CUT = 64
 KCUTS = 4
 INV_TEMP = 10.0
@@ -229,10 +228,10 @@
         c_arrived(dr, 4).wait_recv()
     scores(far, 1 - c)
 
-    sums = jnp.broadcast_to(jnp.sum(den_s[...], axis=1, keepdims=True), (2 * ROWS, 128)).T
-    den_mine[0] = sums[:1, :ROWS]
-    den_mine[1] = sums[:1, ROWS:]
-    den_all[0, z * 2 + c] = sums[:1, :ROWS]
+    sums = jnp.sum(den_s[...].T, axis=0, keepdims=True)
+    den_mine[0] = sums[:, :ROWS]
+    den_mine[1] = sums[:, ROWS:]
+    den_all[0, z * 2 + c] = sums[:, :ROWS]
 
     def d_copy(dz_, dy, dc):
         to_blk = lax.rem(z + dz_, NZ) * 4 + lax.rem(yl + dy, 2) * 2 + lax.rem(c + dc, 2)
@@ -256,12 +255,30 @@
                 if dz_ or dc:
                     go(d_copy(dz_, dy, dc))
 
-    psum = jnp.broadcast_to(jnp.sum(pos_s[...], axis=1, keepdims=True), (2 * ROWS, 128)).T
+    psum = jnp.sum(pos_s[...].T, axis=0, keepdims=True)
     pos_y[...] = psum[:1, ROWS:]
     pcp = copy(pos_y, pos_x, y_send.at[3], y_recv.at[3], ynb)
     go(pcp)
     pos_ref[...] = psum[:1, :ROWS]
     other_z(1)
+    other_z(2)
+
+    def other_half(q):
+        cols = pl.ds(pl.multiple_of(c * half + q * cut, cut), cut)
+        f_t[q * cut : (q + 1) * cut, ROWS : 2 * ROWS] = feat_o[:, cols].T
+
+    def other_rest():
+        other_z(3)
+        for q in (0, 1):
+            go(fc_copy(q))
+        zo_ = u_s[ROWS:]
+        inv_o = lax.rsqrt(jnp.sum(zo_ * zo_, axis=1, keepdims=True) + 1e-06)
+        u_s[ROWS:] = zo_ * inv_o
+        inv_s[ROWS:] = inv_o
+
+    def other_from_sib(q):
+        fc_copy(q).wait_recv()
+        f_t[q * cut : (q + 1) * cut, 3 * ROWS :] = f_sib[1, :, q * cut : (q + 1) * cut].T
 
     docp.wait_recv()
     d_arrived(0, 1, 0).wait_recv()
@@ -286,41 +303,34 @@
         )
         if n == 0:
             acc_s[...] = g
+            other_rest()
         else:
             acc_s[...] += g
-
-    def other_half(q):
-        cols = pl.ds(pl.multiple_of(c * half + q * cut, cut), cut)
-        f_t[q * cut : (q + 1) * cut, ROWS : 2 * ROWS] = feat_o[:, cols].T
-
-    other_z(2)
-    other_z(3)
-    for q in (0, 1):
-        go(fc_copy(q))
-    zo_ = u_s[ROWS:]
-    inv_o = lax.rsqrt(jnp.sum(zo_ * zo_, axis=1, keepdims=True) + 1e-06)
-    u_s[ROWS:] = zo_ * inv_o
-    inv_s[ROWS:] = inv_o
+        if n in (1, 2):
+            other_half(n - 1)
+        if n in (4, 5):
+            other_from_sib(n - 4)
 
     slope = acc_s[...] * INV_TEMP
     u = u_s[...]
     dz = inv_s[...] * (slope - u * jnp.sum(u * slope, axis=1, keepdims=True))
     dz_ref[...] = dz[:ROWS]
     hi = dz.astype(BF16)
+    lo = (dz - hi.astype(F32)).astype(BF16)
     dzh[:2] = hi.reshape(2, ROWS, PROJ)
     xcp = copy(dzh.at[pl.ds(0, 2)], dzh.at[pl.ds(2, 2)], x_send.at[1], x_recv.at[1], sib)
     go(xcp)
-    if LOW:
-        dzl[:2] = (dz - hi.astype(F32)).astype(BF16).reshape(2, ROWS, PROJ)
-        lcp = copy(dzl.at[pl.ds(0, 2)], dzl.at[pl.ds(2, 2)], x_send.at[2], x_recv.at[2], sib)
-        go(lcp)
-    for q in (0, 1):
-        other_half(q)
-        fc_copy(q).wait_recv()
-        f_t[q * cut : (q + 1) * cut, 3 * ROWS :] = f_sib[1, :, q * cut : (q + 1) * cut].T
+    dzl[:2] = lo.reshape(2, ROWS, PROJ)
+    lcp = copy(dzl.at[pl.ds(0, 2)], dzl.at[pl.ds(2, 2)], x_send.at[2], x_recv.at[2], sib)
+
+    for t in range(4):
+        ft = f_t[t * 256 : (t + 1) * 256, : 2 * ROWS]
+        part = jnp.dot(ft, hi, preferred_element_type=F32)
+        part += jnp.dot(ft, lo, preferred_element_type=F32)
+        pf[t] = part.reshape(4, 64, PROJ)
+        if t == 2:
+            go(lcp)
     xcp.wait_recv()
-    if LOW:
-        lcp.wait_recv()
     pl.semaphore_wait(in_sem, 4)
     ycp = copy(dzh.at[1], dzx, y_send.at[4], y_recv.at[4], ynb)
 
@@ -387,10 +397,15 @@
     D3, D7 = (2, 1, 3), (4, 3, 5, 2, 6, 1, 7)
 
     def stage1(t):
-        ft = f_t[t * 256 : (t + 1) * 256, :]
-        part = jnp.dot(ft, dzh[...].reshape(4 * ROWS, PROJ), preferred_element_type=F32)
-        if LOW:
-            part += jnp.dot(ft, dzl[...].reshape(4 * ROWS, PROJ), preferred_element_type=F32)
+        ft = f_t[t * 256 : (t + 1) * 256, 2 * ROWS :]
+        part = pf[t].reshape(256, PROJ)
+        for low in (False, True):
+            if low and t == 2:
+                lcp.wait_recv()
+            if low and t < 2:
+                continue
+            d = (dzl if low else dzh)[2:].reshape(2 * ROWS, PROJ)
+            part = part + jnp.dot(ft, d, preferred_element_type=F32)
         pf[t] = part.reshape(4, 64, PROJ)
         sb1[t] = part.astype(BF16).reshape(4, 64, PROJ)
         for d in D3:

time: 88.8 us -> 87 us (0.980)
  Pallas kernels: 88.1 us -> 86.3 us
    pallas_call x1, Pallas kernels: 85.8 us -> 84 us  [on_device(): pl.pallas_call(kernel, out_shape=(pltpu.VMEM((1, ROWS), F32), pltpu.VMEM(...]
where the time goes in v5:
time: 87 us; the launch traced here: 86.9 us
  Pallas kernels  86.3 us (99%)
    pallas_call x1, Pallas kernels, on_device(): pl.pallas_call(kernel, out_shape=(pltpu.VMEM((1, ROWS), F32), pltpu.VMEM(...  84 us
    pallas_call x1, Pallas kernels, on_device(): pl.pallas_call(finish, out_shape=(jax.ShapeDtypeStruct((1, ROWS), F32), j...  2.28 us

profile of v5, /device:TPU:1, one launch (start us, length us, event | category | flops | bytes accessed | tf_op | source)
XLA Modules:
  0.0 86.9 jit_solution(16851120390556771754)
XLA Ops:
  0.6 84.0 %ntxent.1 = (f32[1,256]{1,0:T(1,128)S(1)}, f32[1,256]{1,0:T(1,128)S(1)}, f32[256,512]{1,0:T(8,128)S(1)}, bf16[2048,512]{1,0:T(8,128)(2,1)S(1)}) custom-call(bf16[256,2048]{1,0:T(8,128)(2,1)} %bitcast.2, bf16[2048,512]{1,0:T(8,128)(2,1)} %w_hbm.1, s32[1,256]{1,0:T(1,128)} %pairs_hbm.1), custom_call_target="tpu_custom_call" | custom-call | tf_op jit(solution)/shard_map/ntxent/pallas_call | solution.py:506
  84.7 2.3 %finish.1 = (f32[1,256]{1,0:T(1,128)}, f32[1,256]{1,0:T(1,128)}, f32[256,512]{1,0:T(8,128)}, f32[2048,512]{1,0:T(8,128)}) custom-call(f32[1,256]{1,0:T(1,128)S(1)} %get-tuple-element.12.pos_in, f32[1,256]{1,0:T(1,128)S(1)} %get-tuple-element.13.lse_in, f32[256,512]{1,0:T(8,128)S(1)} %get-tuple-element.14.dz_in, bf16[2048,512]{1,0:T(8,128)(2,1)S(1)} %get-tuple-element.15.head_in), custom_call_target="tpu_custom_call" | custom-call | tf_op jit(solution)/shard_map/finish/pallas_call | solution.py:571

commit v6 on v5

--- a/solution.py
+++ b/solution.py
@@ -25,7 +25,7 @@
     feat_hbm, w_hbm, pairs_hbm,
     pos_ref, lse_ref, dz_ref, head_ref,
     feat_ref, w_ref, pairs_ref, load_sem,
-    ub_all, ub_r, e_all, u_s, inv_s, pcol_s, den_s, pos_s, den_mine, den_all, den_o, pos_x, pos_y,
+    ub_all, ub_r, e_all, u_s, inv_s, pcol_s, r_s, den_s, pos_s, den_mine, den_all, den_o, pos_x, pos_y,
     acc_s, feat_o, pairs_o, f_sib, f_t, dzh, dzl, dzx, pf, sb1, r1, qf, r2, zb, r3, in_sem,
     z_send, z_recv, y_send, y_recv, fy_send, fy_recv, c_send, c_recv, fc_send, fc_recv,
     d_send, d_recv, x_send, x_recv, s1_send, s1_recv, s2_send, s2_recv, s3_send, s3_recv,
@@ -158,11 +158,11 @@
     own_row = jnp.where(sub < ROWS, blk * ROWS, other_blk * ROWS - ROWS) + sub
 
     def column(row):
-        return jnp.broadcast_to(row, (128, ROWS)).T[:, :1]
-
-    def cols_of(zo, k):
-        first = (zo * 4 + yl * 2 + k) * ROWS
-        return first + lax.broadcasted_iota(jnp.int32, (2 * ROWS, ROWS), 1)
+        return jnp.broadcast_to(row, (128, ROWS)).T
+
+    def cols_of(zo, k, part):
+        first = (zo * 4 + yl * 2 + k) * ROWS + part * 128
+        return first + lax.broadcasted_iota(jnp.int32, (2 * ROWS, 128), 1)
 
     def scores(zo, k):
         lanes = pl.ds(pl.multiple_of(k * ROWS, ROWS), ROWS)
@@ -170,12 +170,16 @@
             ub_r[...].reshape(2 * ROWS, PROJ), ub_all[zo, lanes, :],
             (((1,), (1,)), ((), ())), preferred_element_type=F32,
         )
-        cols = cols_of(zo, k)
-        e = jnp.where(cols == own_row, 0.0, jnp.exp2(s * (INV_TEMP * LOG2E)))
-        e_all[zo, :, lanes] = e
-        p = jnp.where(cols == pcol_s[...], s, 0.0)
-        den_s[...] += e[:, :128] + e[:, 128:]
-        pos_s[...] += p[:, :128] + p[:, 128:]
+        den, pos = den_s[...], pos_s[...]
+        for part in (0, 1):
+            sp = s[:, part * 128 : (part + 1) * 128]
+            cols = cols_of(zo, k, part)
+            e = jnp.where(cols == own_row, 0.0, jnp.exp2(sp * (INV_TEMP * LOG2E)))
+            e_all[zo, :, pl.ds(pl.multiple_of(k * ROWS + part * 128, 128), 128)] = e
+            den += e
+            pos += jnp.where(cols == pcol_s[...], sp, 0.0)
+        den_s[...] = den
+        pos_s[...] = pos
 
     def other_z(k):
         fy_copy(k).wait_recv()
@@ -285,7 +289,8 @@
     me2 = z * 2 + c
     den_own = den_all[0, me2] + den_all[1, me2]
     lse_ref[...] = jnp.log(den_own)
-    r_rows = 1.0 / jnp.concatenate([column(den_own), column(den_o[...] + den_mine[1])], axis=0)
+    r_s[:ROWS] = column(1.0 / den_own)
+    r_s[ROWS:] = column(1.0 / (den_o[...] + den_mine[1]))
     for n, dz_ in enumerate((0, 1, 7, 2, 6, 3, 5, 4)):
         for dy in (0, 1):
             for dc in (0, 1):
@@ -295,9 +300,12 @@
         parts = []
         for k in range(2):
             r_cols = 1.0 / (den_all[0, zo * 2 + k] + den_all[1, zo * 2 + k])
-            e = e_all[zo, :, k * ROWS : (k + 1) * ROWS]
-            h = e * (r_rows + r_cols) - jnp.where(cols_of(zo, k) == pcol_s[...], 2.0, 0.0)
-            parts.append(h.astype(BF16))
+            for part in (0, 1):
+                lanes = slice(part * 128, (part + 1) * 128)
+                e = e_all[zo, :, k * ROWS + part * 128 : k * ROWS + (part + 1) * 128]
+                h = e * (r_s[...] + r_cols[:, lanes])
+                h -= jnp.where(cols_of(zo, k, part) == pcol_s[...], 2.0, 0.0)
+                parts.append(h.astype(BF16))
         g = jnp.dot(
             jnp.concatenate(parts, axis=1), ub_all[zo], preferred_element_type=F32
         )
@@ -523,7 +531,8 @@
             pltpu.VMEM((NZ, 2 * ROWS, 2 * ROWS), F32),
             pltpu.VMEM((2 * ROWS, PROJ), F32),
             pltpu.VMEM((2 * ROWS, 1), F32),
-            pltpu.VMEM((2 * ROWS, 1), jnp.int32),
+            pltpu.VMEM((2 * ROWS, 128), jnp.int32),
+            pltpu.VMEM((2 * ROWS, 128), F32),
             pltpu.VMEM((2 * ROWS, 128), F32),
             pltpu.VMEM((2 * ROWS, 128), F32),
             pltpu.VMEM((2, 1, ROWS), F32),

time: 87 us -> 86.5 us (level)
  no operation moved by 1% of the time
where the time goes in v6:
time: 86.5 us; the launch traced here: 86.4 us
  Pallas kernels  85.8 us (99%)
    pallas_call x1, Pallas kernels, on_device(): pl.pallas_call(kernel, out_shape=(pltpu.VMEM((1, ROWS), F32), pltpu.VMEM(...  83.5 us
    pallas_call x1, Pallas kernels, on_device(): pl.pallas_call(finish, out_shape=(jax.ShapeDtypeStruct((1, ROWS), F32), j...  2.28 us

profile of v6, /device:TPU:1, one launch (start us, length us, event | category | flops | bytes accessed | tf_op | source)
XLA Modules:
  0.0 86.4 jit_solution(16826385244747966829)
XLA Ops:
  0.6 83.5 %ntxent.1 = (f32[1,256]{1,0:T(1,128)S(1)}, f32[1,256]{1,0:T(1,128)S(1)}, f32[256,512]{1,0:T(8,128)S(1)}, bf16[2048,512]{1,0:T(8,128)(2,1)S(1)}) custom-call(bf16[256,2048]{1,0:T(8,128)(2,1)} %bitcast.2, bf16[2048,512]{1,0:T(8,128)(2,1)} %w_hbm.1, s32[1,256]{1,0:T(1,128)} %pairs_hbm.1), custom_call_target="tpu_custom_call" | custom-call | tf_op jit(solution)/shard_map/ntxent/pallas_call | solution.py:514
  84.1 2.3 %finish.1 = (f32[1,256]{1,0:T(1,128)}, f32[1,256]{1,0:T(1,128)}, f32[256,512]{1,0:T(8,128)}, f32[2048,512]{1,0:T(8,128)}) custom-call(f32[1,256]{1,0:T(1,128)S(1)} %get-tuple-element.12.pos_in, f32[1,256]{1,0:T(1,128)S(1)} %get-tuple-element.13.lse_in, f32[256,512]{1,0:T(8,128)S(1)} %get-tuple-element.14.dz_in, bf16[2048,512]{1,0:T(8,128)(2,1)S(1)} %get-tuple-element.15.head_in), custom_call_target="tpu_custom_call" | custom-call | tf_op jit(solution)/shard_map/finish/pallas_call | solution.py:580
